TPU v7x, 256 devices: a whole 4x4x8 slice. The times are simulated.
256 devices in a mesh: ta: 4 (over y_hi, core), ha: 8 (over z), wa: 8 (over y_lo, x).
Axes of the slice: x: 4, y: 4 (y_hi: 2, y_lo: 2; y = y_hi * 2 + y_lo), z: 8, core: 2. Of those that a mesh axis runs over, the one named last changes fastest.
Arguments:
- coarse: bfloat16 [8, 128, 64, 256], P('ta', 'ha', 'wa'), may hold values from -20 to 20
- cache_coarse: bfloat16 [2, 128, 64, 256], P(None, 'ha', 'wa'), may hold values from -6 to 6
- cache_middle: bfloat16 [2, 128, 64, 256], P(None, 'ha', 'wa'), may hold values from -6 to 6
- cache_fine: bfloat16 [2, 256, 128, 256], P(None, 'ha', 'wa'), may hold values from -6 to 6
- coarse_gain: float32 [256], replicated, may hold values from 0.25 to 1.75
- coarse_shift: float32 [256], replicated, may hold values from -2 to 2
- fine_gain: float32 [256], replicated, may hold values from 0.25 to 1.75
- fine_shift: float32 [256], replicated, may hold values from -2 to 2
- coarse_kernel: bfloat16 [3, 3, 3, 256, 256], replicated, may hold values from -0.078125 to 0.078125
- lift_kernel: bfloat16 [3, 3, 3, 256, 256], replicated, may hold values from -0.078125 to 0.078125
- fine_kernel: bfloat16 [3, 3, 3, 256, 128], replicated, may hold values from -0.078125 to 0.078125
- skip_kernel: bfloat16 [256, 128], replicated, may hold values from -0.375 to 0.375
Outputs:
- decoded: bfloat16 [8, 256, 128, 128], P('ta', 'ha', 'wa')
All inputs are finite; a program needn't handle non-finite values.
Results may differ from a plain program's by a relative error of at most 0.008.
Values may be sent and summed in bfloat16 or wider, within the bound.
A program may use at most 128 MiB of HBM per device.

v0:
```python
import jax
import jax.numpy as jnp
from jax import lax
from jax.sharding import PartitionSpec as P

GROUPS = 32


def from_behind(value, axis, steps):
    count = lax.axis_size(axis)
    initial, last = (max(0, -steps), min(count, count - steps))
    return lax.ppermute(value, axis, [(source, source + steps) for source in range(initial, last)])


def padded_2(shard, sides, width):
    for axis, dim in sides:
        count, length = (lax.axis_size(axis), shard.shape[dim])
        up = [(i, (i + 1) % count) for i in range(count - 1)]
        down = [(j, i) for i, j in up]
        last = lax.slice_in_dim(shard, length - width, length, axis=dim)
        initial = lax.slice_in_dim(shard, 0, width, axis=dim)
        before = lax.ppermute(last, axis, up)
        after = lax.ppermute(initial, axis, down)
        shard = jnp.concatenate([before, shard, after], axis=dim)
    return shard


def norm_act(values, gain, shift):
    floats = values.astype(jnp.float32)
    channels = floats.shape[-1]
    group_size = channels // GROUPS
    devices = lax.axis_size("ta") * lax.axis_size("ha") * lax.axis_size("wa")
    entries = floats.shape[0] * floats.shape[1] * floats.shape[2] * group_size * devices

    def grouped(per_channel):
        return jnp.repeat(
            jnp.sum(per_channel.reshape(GROUPS, group_size), axis=1) / entries, group_size
        )

    totals = lax.psum(jnp.sum(floats, axis=(0, 1, 2)), ("ta", "ha", "wa"))
    average = grouped(totals)
    centered_inner = floats - average
    squares = lax.psum(jnp.sum(centered_inner * centered_inner, axis=(0, 1, 2)), ("ta", "ha", "wa"))
    spread = grouped(squares)
    centered = floats - average
    normed = centered * lax.rsqrt(spread + 1e-06) * gain + shift
    return jax.nn.silu(normed).astype(jnp.bfloat16)


def conv_taps(padded, kernel, frames, height, breadth):
    inner = kernel.shape[3]
    outer = kernel.shape[4]
    result = jnp.zeros((frames * height * breadth, outer), jnp.float32)
    for depth_tap in range(3):
        for row_tap in range(3):
            window = jnp.concatenate(
                [
                    padded[
                        depth_tap : depth_tap + frames,
                        row_tap : row_tap + height,
                        col_tap : col_tap + breadth,
                    ]
                    for col_tap in range(3)
                ],
                axis=-1,
            )
            weights = kernel[depth_tap, row_tap].reshape(3 * inner, outer)
            result = result + jnp.dot(
                window.reshape(-1, 3 * inner), weights, preferred_element_type=jnp.float32
            )
    return result.reshape(frames, height, breadth, outer)


def enlarge(values):
    return jnp.repeat(jnp.repeat(values, 2, axis=1), 2, axis=2)


def local(
    coarse,
    cache_coarse,
    cache_middle,
    cache_fine,
    coarse_gain,
    coarse_shift,
    fine_gain,
    fine_shift,
    coarse_kernel,
    lift_kernel,
    fine_kernel,
    skip_kernel,
):
    frames, height, breadth, channels = coarse.shape
    leading = lax.axis_index("ta") == 0
    activated = norm_act(coarse, coarse_gain, coarse_shift)
    before = from_behind(activated, "ta", 1)
    extended = jnp.concatenate([jnp.where(leading, cache_coarse, before), activated], axis=0)
    padded = padded_2(extended, (("ha", 1), ("wa", 2)), 1)
    middle = (
        coarse.astype(jnp.float32) + conv_taps(padded, coarse_kernel, frames, height, breadth)
    ).astype(jnp.bfloat16)
    upsampled = enlarge(middle)
    before_up = from_behind(upsampled, "ta", 1)
    extended_up = jnp.concatenate(
        [jnp.where(leading, enlarge(cache_middle), before_up), upsampled], axis=0
    )
    padded_up = padded_2(extended_up, (("ha", 1), ("wa", 2)), 1)
    lifted = conv_taps(padded_up, lift_kernel, frames, 2 * height, 2 * breadth).astype(jnp.bfloat16)
    fine_act = norm_act(lifted, fine_gain, fine_shift)
    before_fine = from_behind(fine_act, "ta", 1)
    extended_fine = jnp.concatenate([jnp.where(leading, cache_fine, before_fine), fine_act], axis=0)
    padded_fine = padded_2(extended_fine, (("ha", 1), ("wa", 2)), 1)
    skipped = jnp.dot(lifted.reshape(-1, channels), skip_kernel, preferred_element_type=jnp.float32)
    skipped = skipped.reshape(frames, 2 * height, 2 * breadth, skip_kernel.shape[1])
    decoded = skipped + conv_taps(padded_fine, fine_kernel, frames, 2 * height, 2 * breadth)
    return decoded.astype(jnp.bfloat16)


def solution(mesh):
    return jax.shard_map(
        local,
        mesh=mesh,
        in_specs=(
            P("ta", "ha", "wa", None),
            P(None, "ha", "wa", None),
            P(None, "ha", "wa", None),
            P(None, "ha", "wa", None),
            P(),
            P(),
            P(),
            P(),
            P(),
            P(),
            P(),
            P(),
        ),
        out_specs=P("ta", "ha", "wa", None),
        check_vma=False,
    )
```

profile of v0, /device:TPU:1, one launch (start us, length us, event | category | flops | bytes accessed | tf_op | source)
XLA Modules:
  0.0 419.8 jit_solution(629002831731268686)
XLA Ops:
  0.0 1.0 convert_reduce_fusion.1
  1.1 81.5 %psum.28 = f32[32,8]{1,0:T(8,128)S(1)} all-reduce(f32[32,8]{1,0:T(8,128)S(1)} %reshape.148), channel_id=1, replica_groups=mesh['ta'=4,'ha'=8,'wa'=8] {'ta','ha','wa'}, use_global_device_ids=true, to_apply=%region_1.0 | all-reduce | flops 256 | bytes 2048 | tf_op jit(solution)/shard_map/psum | solution.py:40
  82.8 1.0 fusion.22
  83.9 72.8 %psum.29 = f32[32,8]{1,0:T(8,128)S(1)} all-reduce(f32[32,8]{1,0:T(8,128)S(1)} %reshape.149), channel_id=1, replica_groups=mesh['ta'=4,'ha'=8,'wa'=8] {'ta','ha','wa'}, use_global_device_ids=true, to_apply=%region_4.0 | all-reduce | flops 256 | bytes 2048 | tf_op jit(solution)/shard_map/psum | solution.py:43
  156.9 1.0 fusion.30
  158.0 3.6 collective-permute-start
  161.5 1.9 collective-permute-done
  163.5 3.7 collective-permute-start.1
  167.2 1.3 collective-permute-start.2
  168.5 2.3 fusion.35
  170.8 0.8 collective-permute-done.2
  171.8 2.2 collective-permute-start.3
  174.0 1.3 collective-permute-start.4
  175.6 3.8 collective-permute-done.4
  183.7 8.3 %collective-permute-start.5 = (bf16[2,32,16,256]{3,2,1,0:T(8,128)(2,1)S(1)}, bf16[2,32,16,256]{3,2,1,0:T(8,128)(2,1)S(1)}, u32[]{:S(2)}, u32[]{:S(2)}) collective-permute-start(bf16[2,32,16,256]{3,2,1,0:T(8,128)(2,1)S(1)} %reshape.161), channel_id=1, source_target_pairs={{0,64},{64,128},{128,192},{1,65},{65,129},{129,193},{2,66},{66,130... | collective-permute-start | bytes 1572872 | tf_op jit(solution)/shard_map/ppermute | solution.py:12
  192.6 5.5 %collective-permute-done.5 = bf16[2,32,16,256]{3,2,1,0:T(8,128)(2,1)S(1)} collective-permute-done((bf16[2,32,16,256]{3,2,1,0:T(8,128)(2,1)S(1)}, bf16[2,32,16,256]{3,2,1,0:T(8,128)(2,1)S(1)}, u32[]{:S(2)}, u32[]{:S(2)}) %collective-permute-start.5) | collective-permute-done | bytes 524320 | tf_op jit(solution)/shard_map/ppermute | solution.py:12
  198.2 2.3 collective-permute-start.6
  200.5 1.3 collective-permute-start.7
  201.8 3.3 fusion.34
  205.1 1.0 concatenate.234
  206.7 2.2 collective-permute-start.8
  208.9 1.5 collective-permute-start.9
  210.6 4.3 %collective-permute-done.9 = bf16[4,34,1,256]{3,1,2,0:T(8,128)(2,1)S(1)} collective-permute-done((bf16[4,34,1,256]{3,1,2,0:T(8,128)(2,1)S(1)}, bf16[4,34,1,256]{3,1,2,0:T(8,128)(2,1)S(1)}, u32[]{:S(2)}, u32[]{:S(2)}) %collective-permute-start.9) | collective-permute-done | bytes 69664 | tf_op jit(solution)/shard_map/ppermute | solution.py:23
  215.1 1.2 maximum_maximum_fusion
  216.7 0.7 fusion.40
  217.7 0.7 copy-done.3
  218.4 0.6 fusion.50
  219.1 0.6 fusion.51
  220.9 0.9 copy-done.6
  221.7 0.6 convolution_add_fusion.4
  222.7 0.6 convolution_add_fusion.3
  224.3 0.6 fusion.12
  225.5 0.6 fusion.4
  226.1 0.7 convert_reduce_fusion
  226.9 83.0 %psum.30 = f32[32,8]{1,0:T(8,128)S(1)} all-reduce(f32[32,8]{1,0:T(8,128)S(1)} %reshape.170), channel_id=1, replica_groups=mesh['ta'=4,'ha'=8,'wa'=8] {'ta','ha','wa'}, use_global_device_ids=true, to_apply=%region_7.8 | all-reduce | flops 256 | bytes 2048 | tf_op jit(solution)/shard_map/psum | solution.py:40
  310.5 73.3 %psum.31 = f32[32,8]{1,0:T(8,128)S(1)} all-reduce(f32[32,8]{1,0:T(8,128)S(1)} %reshape.171), channel_id=1, replica_groups=mesh['ta'=4,'ha'=8,'wa'=8] {'ta','ha','wa'}, use_global_device_ids=true, to_apply=%region_10.11 | all-reduce | flops 256 | bytes 2048 | tf_op jit(solution)/shard_map/psum | solution.py:43
  384.5 3.7 collective-permute-start.10
  388.2 6.1 %collective-permute-done.10 = bf16[2,32,16,256]{3,2,1,0:T(8,128)(2,1)S(1)} collective-permute-done((bf16[2,32,16,256]{3,2,1,0:T(8,128)(2,1)S(1)}, bf16[2,32,16,256]{3,2,1,0:T(8,128)(2,1)S(1)}, u32[]{:S(2)}, u32[]{:S(2)}) %collective-permute-start.10) | collective-permute-done | bytes 524320 | tf_op jit(solution)/shard_map/ppermute | solution.py:12
  394.3 3.0 collective-permute-start.11
  397.3 1.3 collective-permute-start.12
  398.8 3.2 collective-permute-done.12
  402.5 2.2 collective-permute-start.13
  404.8 1.5 collective-permute-start.14
  406.5 3.4 collective-permute-done.14
  410.1 1.2 maximum_maximum_fusion.1
  411.7 0.7 fusion.38
  415.3 0.6 convolution_add_fusion.10
  418.8 1.0 fusion.15
  (130 shorter events, 19.2 us)
Async XLA Ops:
  0.0 418.8 %copy-start = (bf16[256,128]{1,0:T(8,128)(2,1)S(1)}, bf16[256,128]{1,0:T(8,128)(2,1)}, u32[]{:S(2)}) copy-start(bf16[256,128]{1,0:T(8,128)(2,1)} %param.23) | copy-start | bytes 196612
  158.0 5.5 %collective-permute-start = (bf16[2,16,8,256]{3,2,1,0:T(8,128)(2,1)S(1)}, bf16[2,16,8,256]{3,2,1,0:T(8,128)(2,1)S(1)}, u32[]{:S(2)}, u32[]{:S(2)}) collective-permute-start(bf16[2,16,8,256]{3,2,1,0:T(8,128)(2,1)S(1)} %fusion.30), channel_id=1, source_target_pairs={{0,64},{64,128},{128,192},{1,65},{65,129},{129,193},{2,66},{66,130... | collective-permute-start | bytes 393224 | tf_op jit(solution)/shard_map/ppermute | solution.py:12
  163.5 7.3 %collective-permute-start.1 = (bf16[4,1,8,256]{3,2,1,0:T(8,128)(2,1)S(1)}, bf16[4,1,8,256]{3,2,1,0:T(8,128)(2,1)S(1)}, u32[]{:S(2)}, u32[]{:S(2)}) collective-permute-start(bf16[4,1,8,256]{3,2,1,0:T(8,128)(2,1)S(1)} %get-tuple-element.131), channel_id=1, source_target_pairs={{0,8},{8,16},{16,24},{24,32},{32,40},{40,48},{48,56},{1,9},{9,17},... | collective-permute-start | bytes 49160 | tf_op jit(solution)/shard_map/ppermute | solution.py:22
  167.2 4.5 %collective-permute-start.2 = (bf16[4,1,8,256]{3,2,1,0:T(8,128)(2,1)S(1)}, bf16[4,1,8,256]{3,2,1,0:T(8,128)(2,1)S(1)}, u32[]{:S(2)}, u32[]{:S(2)}) collective-permute-start(bf16[4,1,8,256]{3,2,1,0:T(8,128)(2,1)S(1)} %get-tuple-element.132), channel_id=1, source_target_pairs={{8,0},{16,8},{24,16},{32,24},{40,32},{48,40},{56,48},{9,1},{17,9},... | collective-permute-start | bytes 49160 | tf_op jit(solution)/shard_map/ppermute | solution.py:23
  171.8 3.9 collective-permute-start.3
  174.0 5.5 %collective-permute-start.4 = (bf16[4,18,1,256]{3,2,1,0:T(2,128)(2,1)S(1)}, bf16[4,18,1,256]{3,2,1,0:T(2,128)(2,1)S(1)}, u32[]{:S(2)}, u32[]{:S(2)}) collective-permute-start(bf16[4,18,1,256]{3,2,1,0:T(2,128)(2,1)S(1)} %get-tuple-element.122), channel_id=1, source_target_pairs={{1,0},{2,1},{3,2},{4,3},{5,4},{6,5},{7,6},{9,8},{10,9},{11,10},{12... | collective-permute-start | bytes 110600 | tf_op jit(solution)/shard_map/ppermute | solution.py:23
  182.2 0.9 copy-start.1
  182.8 9.3 %copy-start.10 = (bf16[2,16,8,256]{3,2,1,0:T(8,128)(2,1)S(1)}, bf16[2,16,8,256]{3,2,1,0:T(8,128)(2,1)}, u32[]{:S(2)}) copy-start(bf16[2,16,8,256]{3,2,1,0:T(8,128)(2,1)} %param.14) | copy-start | bytes 393220
  183.7 14.5 %collective-permute-start.5 = (bf16[2,32,16,256]{3,2,1,0:T(8,128)(2,1)S(1)}, bf16[2,32,16,256]{3,2,1,0:T(8,128)(2,1)S(1)}, u32[]{:S(2)}, u32[]{:S(2)}) collective-permute-start(bf16[2,32,16,256]{3,2,1,0:T(8,128)(2,1)S(1)} %reshape.161), channel_id=1, source_target_pairs={{0,64},{64,128},{128,192},{1,65},{65,129},{129,193},{2,66},{66,130... | collective-permute-start | bytes 1572872 | tf_op jit(solution)/shard_map/ppermute | solution.py:12
  198.2 7.9 %collective-permute-start.6 = (bf16[4,1,16,256]{3,2,1,0:T(8,128)(2,1)S(1)}, bf16[4,1,16,256]{3,2,1,0:T(8,128)(2,1)S(1)}, u32[]{:S(2)}, u32[]{:S(2)}) collective-permute-start(bf16[4,1,16,256]{3,2,1,0:T(8,128)(2,1)S(1)} %get-tuple-element.94), channel_id=1, source_target_pairs={{0,8},{8,16},{16,24},{24,32},{32,40},{40,48},{48,56},{1,9},{9,17},... | collective-permute-start | bytes 98312 | tf_op jit(solution)/shard_map/ppermute | solution.py:22
  200.5 5.6 %collective-permute-start.7 = (bf16[4,1,16,256]{3,2,1,0:T(8,128)(2,1)S(1)}, bf16[4,1,16,256]{3,2,1,0:T(8,128)(2,1)S(1)}, u32[]{:S(2)}, u32[]{:S(2)}) collective-permute-start(bf16[4,1,16,256]{3,2,1,0:T(8,128)(2,1)S(1)} %get-tuple-element.95), channel_id=1, source_target_pairs={{8,0},{16,8},{24,16},{32,24},{40,32},{48,40},{56,48},{9,1},{17,9},... | collective-permute-start | bytes 98312 | tf_op jit(solution)/shard_map/ppermute | solution.py:23
  206.7 3.8 collective-permute-start.8
  208.9 6.1 %collective-permute-start.9 = (bf16[4,34,1,256]{3,1,2,0:T(8,128)(2,1)S(1)}, bf16[4,34,1,256]{3,1,2,0:T(8,128)(2,1)S(1)}, u32[]{:S(2)}, u32[]{:S(2)}) collective-permute-start(bf16[4,34,1,256]{3,1,2,0:T(8,128)(2,1)S(1)} %copy.19), channel_id=1, source_target_pairs={{1,0},{2,1},{3,2},{4,3},{5,4},{6,5},{7,6},{9,8},{10,9},{11,10},{12... | collective-permute-start | bytes 208904 | tf_op jit(solution)/shard_map/ppermute | solution.py:23
  217.4 1.0 copy-start.3
  220.7 1.0 copy-start.6
  221.7 1.0 copy-start.5
  222.7 1.0 copy-start.4
  224.3 1.0 copy-start.8
  224.3 1.1 copy-start.9
  226.0 158.0 %copy-start.11 = (f32[256]{0:T(256)S(1)}, f32[256]{0:T(256)}, u32[]{:S(2)}) copy-start(f32[256]{0:T(256)} %param.19) | copy-start | bytes 3076
  226.1 158.0 %copy-start.12 = (f32[256]{0:T(256)S(1)}, f32[256]{0:T(256)}, u32[]{:S(2)}) copy-start(f32[256]{0:T(256)} %param.18) | copy-start | bytes 3076
  226.8 167.5 %copy-start.7 = (bf16[2,32,16,256]{3,2,1,0:T(8,128)(2,1)S(1)}, bf16[2,32,16,256]{3,2,1,0:T(8,128)(2,1)}, u32[]{:S(2)}) copy-start(bf16[2,32,16,256]{3,2,1,0:T(8,128)(2,1)} %param.15) | copy-start | bytes 1572868
  384.4 14.2 %copy-start.2 = (bf16[3,3,3,256,128]{4,3,2,1,0:T(8,128)(2,1)S(1)}, bf16[3,3,3,256,128]{4,3,2,1,0:T(8,128)(2,1)}, u32[]{:S(2)}) copy-start(bf16[3,3,3,256,128]{4,3,2,1,0:T(8,128)(2,1)} %param.22) | copy-start | bytes 5308420
  384.5 9.8 %collective-permute-start.10 = (bf16[2,32,16,256]{3,2,1,0:T(8,128)(2,1)S(1)}, bf16[2,32,16,256]{3,2,1,0:T(8,128)(2,1)S(1)}, u32[]{:S(2)}, u32[]{:S(2)}) collective-permute-start(bf16[2,32,16,256]{3,2,1,0:T(8,128)(2,1)S(1)} %multiply_convert_fusion), channel_id=1, source_target_pairs={{0,64},{64,128},{128,192},{1,65},{65,129},{129,193},{2,66},{66,130... | collective-permute-start | bytes 1572872 | tf_op jit(solution)/shard_map/ppermute | solution.py:12
  394.3 4.5 %collective-permute-start.11 = (bf16[4,1,16,256]{3,2,1,0:T(8,128)(2,1)S(1)}, bf16[4,1,16,256]{3,2,1,0:T(8,128)(2,1)S(1)}, u32[]{:S(2)}, u32[]{:S(2)}) collective-permute-start(bf16[4,1,16,256]{3,2,1,0:T(8,128)(2,1)S(1)} %get-tuple-element.90), channel_id=1, source_target_pairs={{0,8},{8,16},{16,24},{24,32},{32,40},{40,48},{48,56},{1,9},{9,17},... | collective-permute-start | bytes 98312 | tf_op jit(solution)/shard_map/ppermute | solution.py:22
  397.3 4.7 %collective-permute-start.12 = (bf16[4,1,16,256]{3,2,1,0:T(8,128)(2,1)S(1)}, bf16[4,1,16,256]{3,2,1,0:T(8,128)(2,1)S(1)}, u32[]{:S(2)}, u32[]{:S(2)}) collective-permute-start(bf16[4,1,16,256]{3,2,1,0:T(8,128)(2,1)S(1)} %get-tuple-element.91), channel_id=1, source_target_pairs={{8,0},{16,8},{24,16},{32,24},{40,32},{48,40},{56,48},{9,1},{17,9},... | collective-permute-start | bytes 98312 | tf_op jit(solution)/shard_map/ppermute | solution.py:23
  402.5 3.9 collective-permute-start.13
  404.8 5.2 %collective-permute-start.14 = (bf16[4,34,1,256]{3,1,2,0:T(8,128)(2,1)S(1)}, bf16[4,34,1,256]{3,1,2,0:T(8,128)(2,1)S(1)}, u32[]{:S(2)}, u32[]{:S(2)}) collective-permute-start(bf16[4,34,1,256]{3,1,2,0:T(8,128)(2,1)S(1)} %copy.23), channel_id=1, source_target_pairs={{1,0},{2,1},{3,2},{4,3},{5,4},{6,5},{7,6},{9,8},{10,9},{11,10},{12... | collective-permute-start | bytes 208904 | tf_op jit(solution)/shard_map/ppermute | solution.py:23
where the time goes:
time: 426 us; the launch traced here: 420 us
  blocking collectives  311 us (73%)
  starting transfers between devices  39.2 us (9%)
  waiting for transfers between devices  29.4 us (7%)
  local copies, waits for them, and re-layouts  15.6 us (4%)
  matrix products  14 us (3%)
  other arithmetic  10.1 us (2%)
    psum x2, blocking collectives, norm_act(): totals = lax.psum(jnp.sum(floats, axis=(0, 1, 2)), ('ta', 'ha', 'wa'))  164 us
    psum x2, blocking collectives, norm_act(): lax.psum(jnp.sum(centered_inner * centered_inner, axis=(0, 1, 2)), ('ta',...  146 us
    ppermute x3, starting transfers between devices, from_behind(): lax.ppermute(value, axis, [(source, source + steps) for source in range(i...  15.6 us
    ppermute x6, waiting for transfers between devices, padded_2(): after = lax.ppermute(initial, axis, down)  15.5 us
    ppermute x6, starting transfers between devices, padded_2(): before = lax.ppermute(last, axis, up)  15.5 us
    ppermute x3, waiting for transfers between devices, from_behind(): lax.ppermute(value, axis, [(source, source + steps) for source in range(i...  13.6 us
    dot_general x27, matrix products, conv_taps(): jnp.dot(window.reshape(-1, 3 * inner), weights, preferred_element_type=jn...  13 us
  transfers between devices with their start and end apart: 15, of which 9 were waited for; matrix products, arithmetic and copies ran while one was open for 2% of the time, Pallas kernels for 0%

commit v1 on v0

v1 whole, which is shorter than its diff:
```python
import functools

import jax
import jax.numpy as jnp
from jax import lax
from jax.experimental import pallas as pl
from jax.experimental.pallas import tpu as pltpu
from jax.sharding import PartitionSpec as P

GROUPS = 32
EPS = 1e-06
MESH = pl.DeviceIdType.MESH
F32 = jnp.float32
BF16 = jnp.bfloat16


def rolled(value, shift):
    size = value.shape[0]
    shift = shift % size
    return value if shift == 0 else pltpu.roll(value, shift, 0)


def put(ref, start, value):
    width = ref.shape[-1]
    for part in range(value.shape[1] // width):
        ref[part, pl.ds(start, value.shape[0]), :] = value[:, part * width : (part + 1) * width]


def take(ref, start, stride=1, parts=None):
    at = pl.ds(start, 16) if stride == 1 else pl.ds(start, 16, stride=stride)
    return jnp.concatenate([ref[part, at, :] for part in range(parts or ref.shape[0])], axis=1)


def body(
    sizes,
    coarse_hbm, cache_coarse_hbm, cache_middle_hbm, cache_fine_hbm,
    coarse_gain, coarse_shift, fine_gain, fine_shift,
    coarse_kernel, lift_kernel, fine_kernel, skip_kernel,
    out_ref, affine,
    cb, ccb, cmb, cfb, xf, cff, xt, ts, xtf, ss, sr, saf, act_a, acc1, w1, lk, w2, w3, skw,
    cm, cs, cfs, mt, mid_g, gf, acc2, lt, lf, acc3, back, ar_src, ar_recv,
    local_sem, ar_send, ar_got, send_sem, recv_sem,
):
    nt, nh, nw, C, C1 = sizes
    half = gf.shape[0] // 2
    ta, ha, wa = lax.axis_index("ta"), lax.axis_index("ha"), lax.axis_index("wa")
    row16 = lax.broadcasted_iota(jnp.int32, (16, C), 0)
    row16w = lax.broadcasted_iota(jnp.int32, (16, 2 * C), 0)
    first_w, last_w, first_h, last_h = wa == 0, wa == nw - 1, ha == 0, ha == nh - 1

    def near(t=0, h=0, w=0):
        where = {}
        if t:
            where["ta"] = lax.rem(ta + (t + nt), nt)
        if h:
            where["ha"] = lax.rem(ha + (h + nh), nh)
        if w:
            where["wa"] = lax.rem(wa + (w + nw), nw)
        return where

    loads = []

    def load(src, dst):
        copy = pltpu.make_async_copy(src, dst, local_sem.at[len(loads)])
        copy.start()
        loads.append(copy)
        return copy

    get_coarse = load(coarse_hbm, cb)
    barrier = pltpu.get_barrier_semaphore()
    friends = [near(w=d) for d in range(1, nw)] + [near(h=d) for d in range(1, nh)] + [near(t=d) for d in range(1, nt)]
    friends += [near(t=-1, w=1), near(t=-1, w=-1)]
    for friend in friends:
        pl.semaphore_signal(barrier, inc=1, device_id=friend, device_id_type=MESH)
    get_cc = load(cache_coarse_hbm, ccb)
    get_cm = load(cache_middle_hbm, cmb)
    get_cf = load(cache_fine_hbm, cfb)
    get_lk = load(lift_kernel, lk)
    get_w1 = [
        load(coarse_kernel.at[dt, dh, dw], w1.at[dt, (3 * dw + dh) * C : (3 * dw + dh + 1) * C])
        for dt in range(3) for dh in range(3) for dw in range(3)
    ]
    get_w3 = [
        load(fine_kernel.at[dt, dh], w3.at[3 * dt : 3 * dt + 3, (a + dh) * C : (a + dh + 1) * C, a * C1 : (a + 1) * C1])
        for dt in range(3) for dh in range(3) for a in range(2)
    ]
    get_affine = [load(ref, affine.at[i]) for i, ref in enumerate((coarse_gain, coarse_shift, fine_gain, fine_shift))]
    get_skip = [load(skip_kernel, skw.at[a * C : (a + 1) * C, a * C1 : (a + 1) * C1]) for a in range(2)]

    get_coarse.wait()
    flat = cb[...].astype(F32)
    put(xf, 0, flat)
    count = flat.shape[0]
    mean = jnp.sum(flat, axis=0, keepdims=True) / count
    centred = flat - mean
    ar_src[0, 0] = jnp.zeros((8, C), F32)
    ar_src[0, 0, 0:1, :] = mean
    ar_src[0, 0, 1:2, :] = jnp.sum(centred * centred, axis=0, keepdims=True) / count
    get_cc.wait()
    pl.semaphore_wait(barrier, len(friends))

    def message(index, src, dst, where):
        return pltpu.make_async_remote_copy(
            src_ref=src, dst_ref=dst, send_sem=send_sem.at[index], recv_sem=recv_sem.at[index],
            device_id=where, device_id_type=MESH,
        )

    stages = ((("w", nw), 0), (("h", nh), nw - 1), (("t", nt), nw - 1 + nh - 1))

    def ar_copies(which, stage):
        (axis, n), base = stages[stage]
        return [
            pltpu.make_async_remote_copy(
                src_ref=ar_src.at[which, stage], dst_ref=ar_recv.at[which, base + d - 1],
                send_sem=ar_send.at[which, base + d - 1], recv_sem=ar_got.at[which, base + d - 1],
                device_id=near(**{axis: d}), device_id_type=MESH,
            )
            for d in range(1, n)
        ]

    def ar_start(which, stage):
        for copy in ar_copies(which, stage):
            copy.start()

    def ar_finish(which, stage):
        (_, n), base = stages[stage]
        for copy in ar_copies(which, stage):
            copy.wait_recv()
        tiles = [ar_src[which, stage]] + [ar_recv[which, base + d - 1] for d in range(1, n)]
        average = functools.reduce(jnp.add, tiles) / n
        spread = functools.reduce(jnp.add, [(tile - average) * (tile - average) for tile in tiles]) / n
        rows = lax.broadcasted_iota(jnp.int32, (8, C), 0)
        return average + jnp.where(rows == 1, pltpu.roll(spread, 1, 0), 0.0)

    def ar_next(which, stage):
        ar_src[which, stage + 1] = ar_finish(which, stage)
        ar_start(which, stage + 1)

    size = C // GROUPS
    width = xf.shape[-1]

    def group_mean(value):
        lane_of = lax.broadcasted_iota(jnp.int32, (8, width), 1)
        parts = []
        for part in range(C // width):
            x = jnp.broadcast_to(value[:, part * width : (part + 1) * width], (8, width))
            step = 1
            while step < size:
                x = x + jnp.where((lane_of & step) == 0, pltpu.roll(x, width - step, 1), pltpu.roll(x, step, 1))
                step *= 2
            parts.append(x[0:1])
        return jnp.concatenate(parts, axis=1) / size

    def normaliser(which, gain, shift):
        tile = ar_finish(which, 2)
        mean, variance = tile[0:1], tile[1:2]
        grouped = group_mean(mean)
        away = mean - grouped
        mean, variance = grouped, group_mean(variance + away * away)
        half_scale = 0.5 * (gain * lax.rsqrt(variance + EPS))
        half_shift = 0.5 * shift

        def act(x, mean=mean, half_scale=half_scale, half_shift=half_shift):
            half = (x - mean) * half_scale + half_shift
            return half + half * jnp.tanh(half)

        return act, mean, half_scale, half_shift

    ar_start(0, 0)
    for f in range(2):
        for c in range(8):
            xt[2 + f, 2 + c] = take(xf, f * 128 + c, 8).astype(BF16)

    @pl.when(ta == nt - 1)
    def _():
        put(xf, 0, ccb[...].astype(F32))
        for f in range(2):
            for c in range(8):
                ts[f, c] = take(xf, f * 128 + c, 8).astype(BF16)

    @pl.when(ta != nt - 1)
    def _():
        ts[...] = xt[2:4, 2:10]

    first = [
        message(0, ts, xt.at[0:2, 2:10], near(t=1)),
        message(1, xt.at[2:4, 8:10], xt.at[2:4, 0:2], near(w=1)),
        message(2, xt.at[2:4, 2:4], xt.at[2:4, 10:12], near(w=-1)),
        message(3, ts.at[:, 6:8], xt.at[0:2, 0:2], near(t=1, w=1)),
        message(4, ts.at[:, 0:2], xt.at[0:2, 10:12], near(t=1, w=-1)),
    ]
    for copy in first:
        copy.start()

    cm_first = [
        message(5, cm.at[:, 8:9], cm.at[:, 0:1], near(w=1)),
        message(6, cm.at[:, 1:2], cm.at[:, 9:10], near(w=-1)),
    ]
    cf_first = [
        message(7, lt.at[:, 0:2, 8:9, :, 0:C], lt.at[:, 0:2, 0:1, :, 0:C], near(w=1)),
        message(8, lt.at[:, 0:2, 0:1, :, C : 2 * C], lt.at[:, 0:2, 8:9, :, C : 2 * C], near(w=-1)),
    ]
    cm_second = [
        message(11, cs.at[:, 0:1], cm.at[:, 11:12], near(h=-1)),
        message(12, cs.at[:, 1:2], cm.at[:, 10:11], near(h=1)),
    ]
    cf_second = [
        message(13, cfs.at[0], lt.at[0, 0:2, 9:10], near(h=-1)),
        message(14, cfs.at[1], lt.at[1, 0:2, 9:10], near(h=1)),
    ]

    get_cm.wait()

    @pl.when(ta < 2)
    def _():
        put(xf, 0, cmb[...].astype(F32))
        for f in range(2):
            for c in range(8):
                cm[f, 1 + c] = take(xf, f * 128 + c, 8).astype(BF16)
        for copy in cm_first:
            copy.start()

    for dt in range(3):
        for dw in range(3):
            w3[3 * dt + dw, 3 * C : 4 * C, 0:C1] = jnp.zeros((C, C1), BF16)
            w3[3 * dt + dw, 0:C, C1 : 2 * C1] = jnp.zeros((C, C1), BF16)
    skw[0:C, C1 : 2 * C1] = jnp.zeros((C, C1), BF16)
    skw[C : 2 * C, 0:C1] = jnp.zeros((C, C1), BF16)
    def fold(i, carry):
        dt, r = i // (C // 16), pl.multiple_of(lax.rem(i, C // 16) * 16, 16)
        taps = [[lk[dt, dh, dw, pl.ds(r, 16), :].astype(F32) for dw in range(3)] for dh in range(3)]
        for a in range(2):
            for k in range(2):
                if a == 0:
                    line = taps[0] if k == 0 else [taps[1][d] + taps[2][d] for d in range(3)]
                else:
                    line = [taps[0][d] + taps[1][d] for d in range(3)] if k == 0 else taps[2]
                wide = ((line[0] + line[1], line[2]), (line[0], line[1] + line[2]))
                for b in range(2):
                    for j in range(2):
                        w2[a, dt, pl.ds((2 * j + k) * C + r, 16), b * C : (b + 1) * C] = wide[b][j].astype(BF16)
        return carry

    get_lk.wait()
    ar_next(0, 0)
    lax.fori_loop(0, 3 * (C // 32), fold, 0)
    ar_next(0, 1)

    for copy in first:
        copy.wait_recv()

    def widen(i, carry):
        f, c = i // 12, i % 12
        put(xtf, pl.multiple_of(i * 16, 16), xt[f, c].astype(F32))
        return carry

    lax.fori_loop(0, 48, widen, 0, unroll=8)
    for f in range(4):
        for side, rows in enumerate(((0, 1), (14, 15))):
            for k, row in enumerate(rows):
                ss[side, f, k] = take(xtf, f * 192 + row, 16).astype(BF16)
    second = [
        message(9, ss.at[0], sr.at[1], near(h=-1)),
        message(10, ss.at[1], sr.at[0], near(h=1)),
    ]
    for copy in second:
        copy.start()

    @pl.when(ta < 2)
    def _():
        for copy in cm_first:
            copy.wait_recv()
        for f in range(2):
            for c in range(10):
                put(gf, 16 * c, cm[f, c].astype(F32))
            cs[f, 0] = take(gf, 0, 16, half).astype(BF16)
            cs[f, 1] = take(gf, 15, 16, half).astype(BF16)
        for copy in cm_second:
            copy.start()

    lax.fori_loop(3 * (C // 32), 3 * (C // 16), fold, 0)
    for copy in get_w1 + get_w3 + get_skip + get_affine:
        copy.wait()

    for copy in second:
        copy.wait_recv()
    act, *_ = normaliser(0, affine[0], affine[1])

    cols = lax.broadcasted_iota(jnp.int32, (16, C), 0)

    def strips_of(f):
        raw = jnp.logical_and(ta == 0, f < 2)
        for side in range(2):
            outside = first_h if side == 0 else last_h
            for k in range(2):
                x = sr[side, f, k].astype(F32)
                y = jnp.where(raw, x, act(x)) if f < 2 else act(x)
                gone = jnp.logical_or(jnp.logical_and(first_w, cols < 2), jnp.logical_and(last_w, cols >= 10))
                saf[f, side, k] = jnp.where(jnp.logical_or(outside, gone), 0.0, y)

    def act_coarse(f):
        strips_of(f)
        for c in range(12):
            at = f * 192 + c * 16
            x = take(xtf, at)
            x = jnp.where(ta == 0, x, act(x)) if f < 2 else act(x)
            if c < 2:
                x = jnp.where(first_w, 0.0, x)
            if c >= 10:
                x = jnp.where(last_w, 0.0, x)
            put(xtf, at, x)
            above = jnp.where(row16 == 0, saf[f, 0, 1, c : c + 1, :], rolled(x, 1))
            below = jnp.where(row16 == 15, saf[f, 1, 0, c : c + 1, :], rolled(x, -1))
            act_a[f, c, :, 0:C] = above.astype(BF16)
            act_a[f, c, :, C : 2 * C] = x.astype(BF16)
            act_a[f, c, :, 2 * C : 3 * C] = below.astype(BF16)
        top = take(xtf, f * 192, 16)
        bottom = take(xtf, f * 192 + 15, 16)
        for side, lines in enumerate(((saf[f, 0, 0], saf[f, 0, 1], top), (bottom, saf[f, 1, 0], saf[f, 1, 1]))):
            for dw in range(3):
                for dh in range(3):
                    act_a[f, 12 + 2 * dw + side, :, dh * C : (dh + 1) * C] = rolled(lines[dh], -dw).astype(BF16)

    def conv_coarse(g):
        lhs = jnp.concatenate(
            [
                jnp.concatenate([act_a[g, dw : dw + 10], act_a[g, 12 + 2 * dw : 14 + 2 * dw]], axis=0)
                for dw in range(3)
            ],
            axis=-1,
        ).reshape(12 * 16, 9 * C)
        for f in range(2):
            if 0 <= g - f <= 2:
                part = jnp.dot(lhs, w1[g - f], preferred_element_type=F32).reshape(12, 16, C)
                acc1[f] = part if g == f else acc1[f] + part

    def finish_middle(f):
        for c in range(10):
            y = xt[2 + f, 1 + c].astype(F32) + acc1[f, c]
            if c == 0:
                y = jnp.where(first_w, 0.0, y)
            if c == 9:
                y = jnp.where(last_w, 0.0, y)
            mt[4 + f, c] = y.astype(BF16)
        gone = (cols > 9) | (first_w & (cols == 0)) | (last_w & (cols == 9))
        for side in range(2):
            y = rolled(sr[side, 2 + f, 1 - side].astype(F32), -1) + acc1[f, 10 + side]
            y = jnp.where(jnp.logical_or(gone, first_h if side == 0 else last_h), 0.0, y)
            mt[4 + f, 10 + side] = y.astype(BF16)

    to_next = [message(15 + f, mt.at[4 + f : 5 + f], mt.at[2 + f : 3 + f], near(t=1)) for f in range(2)]

    def send_middle(f):
        finish_middle(f)

        @pl.when(ta < nt - 1)
        def _():
            to_next[f].start()

    act_coarse(0)
    for g in range(4):
        if g < 3:
            act_coarse(g + 1)
        conv_coarse(g)
        if g >= 2:
            send_middle(g - 2)

    to_second = message(17, mt.at[4:6], mt.at[0:2], near(t=2))
    by_second = message(17, mt.at[2:4], mt.at[0:2], near(t=1))

    def prepare(g):
        top = mt[g, 10].astype(F32)
        bottom = mt[g, 11].astype(F32)
        for c in range(10):
            x = mt[g, c].astype(F32)
            put(gf, 16 * c, x)
            mid_g[g, c, :, 0:C] = jnp.where(row16 == 0, top[c : c + 1], rolled(x, 1)).astype(BF16)
            mid_g[g, c, :, C : 2 * C] = mt[g, c]
            mid_g[g, c, :, 2 * C : 3 * C] = jnp.where(row16 == 15, bottom[c : c + 1], rolled(x, -1)).astype(BF16)
        row_top = take(gf, 0, 16, half)
        row_bottom = take(gf, 15, 16, half)
        for j in range(2):
            mid_g[g, 10 + j, :, 0:C] = rolled(row_bottom, -j).astype(BF16)
            mid_g[g, 10 + j, :, C : 2 * C] = rolled(bottom, -j).astype(BF16)
            mid_g[g, 12 + j, :, C : 2 * C] = rolled(top, -j).astype(BF16)
            mid_g[g, 12 + j, :, 2 * C : 3 * C] = rolled(row_top, -j).astype(BF16)

    def lift_part(a, dt, g, frames):
        lanes = slice(a * C, (a + 2) * C)
        lhs = jnp.concatenate(
            [
                jnp.concatenate(
                    [mid_g[g : g + frames, j : j + 9, :, lanes], mid_g[g : g + frames, 10 + 2 * a + j : 11 + 2 * a + j, :, lanes]],
                    axis=1,
                )
                for j in range(2)
            ],
            axis=-1,
        ).reshape(frames * 10 * 16, 4 * C)
        part = jnp.dot(lhs, w2[a, dt], preferred_element_type=F32)
        return part.reshape(frames, 10, 16, 2 * C)

    def cached_middle(at):
        gone = (cols > 9) | (first_w & (cols == 0)) | (last_w & (cols == 9))
        for f in range(2):
            mt[at + f, 1:9] = cm[f, 1:9]
            mt[at + f, 0] = jnp.where(first_w, 0.0, cm[f, 0].astype(F32)).astype(BF16)
            mt[at + f, 9] = jnp.where(last_w, 0.0, cm[f, 9].astype(F32)).astype(BF16)
            for side in range(2):
                outside = jnp.logical_or(gone, first_h if side == 0 else last_h)
                mt[at + f, 10 + side] = jnp.where(outside, 0.0, cm[f, 10 + side].astype(F32)).astype(BF16)

    prepare(4)
    prepare(5)
    for a in range(2):
        acc2[a] = lift_part(a, 2, 4, 2)
        acc2[a, 1:2] += lift_part(a, 1, 4, 1)

    @pl.when(ta == 0)
    def _():
        for copy in cm_second:
            copy.wait_recv()
        cached_middle(2)

    @pl.when(ta > 0)
    def _():
        for copy in to_next:
            copy.wait_recv()

    @pl.when(ta == 2)
    def _():
        by_second.start()

    prepare(2)
    prepare(3)
    for a in range(2):
        acc2[a] += lift_part(a, 0, 2, 2)
        acc2[a, 0:1] += lift_part(a, 1, 3, 1)
        lt[a, 2:4] = acc2[a].astype(BF16)

    @pl.when(ta == 0)
    def _():
        to_second.start()

    def own_sums(fn):
        total = jnp.zeros((16, C), F32)
        for a in range(2):
            for f in range(2):
                for p in range(9):
                    for b in range(2):
                        if (p, b) in ((0, 0), (8, 1)):
                            continue
                        total = total + fn(lt[a, 2 + f, p, :, b * C : (b + 1) * C].astype(F32))
        return jnp.sum(total, axis=0, keepdims=True) / (2 * 2 * 16 * 16)

    mean = own_sums(lambda x: x)
    ar_src[1, 0] = jnp.zeros((8, C), F32)
    ar_src[1, 0, 0:1, :] = mean
    ar_src[1, 0, 1:2, :] = own_sums(lambda x: (x - mean) * (x - mean))
    ar_start(1, 0)

    def lift_before_new(a):
        acc2[a] = lift_part(a, 2, 2, 2)
        acc2[a, 1:2] += lift_part(a, 1, 2, 1)

    def lift_before_old(a):
        acc2[a] += lift_part(a, 0, 0, 2)
        lt[a, 0:1] = (acc2[a, 0:1] + lift_part(a, 1, 1, 1)).astype(BF16)
        lt[a, 1:2] = acc2[a, 1:2].astype(BF16)

    @pl.when(ta > 0)
    def _():
        lift_before_new(0)
        lift_before_new(1)

    get_cf.wait()

    @pl.when(ta == 0)
    def _():
        put(cff, 0, cfb[...].astype(F32))
        for f in range(2):
            for c in range(16):
                p, b = (c + 1) // 2, (c + 1) % 2
                for a in range(2):
                    lt[a, f, p, :, b * C : (b + 1) * C] = take(cff, f * 512 + a * 16 + c, 32).astype(BF16)
        for copy in cf_first:
            copy.start()

    ar_next(1, 0)

    @pl.when(ta == 0)
    def _():
        for copy in cf_first:
            copy.wait_recv()
        for f in range(2):
            for a, row in ((0, 0), (1, 15)):
                for p in range(9):
                    put(gf, 16 * p, lt[a, f, p].astype(F32))
                cfs[a, f, 0] = take(gf, row, 16).astype(BF16)
        for copy in cf_second:
            copy.start()

    for b in range(2):
        lhs = jnp.concatenate([lt[a, 2:4, 1 - b : 9 - b, :, b * C : (b + 1) * C] for a in range(2)], axis=-1)
        part = jnp.dot(lhs.reshape(2 * 8 * 16, 2 * C), skw[...], preferred_element_type=F32)
        acc3[:, :, 1 - b] = part.reshape(2, 8, 16, 2 * C1)

    ar_next(1, 1)

    @pl.when(ta == 1)
    def _():
        for copy in cm_second:
            copy.wait_recv()
        cached_middle(0)

    @pl.when(ta > 1)
    def _():
        to_second.wait_recv()

    @pl.when(ta > 0)
    def _():
        prepare(0)
        prepare(1)
        lift_before_old(0)
        lift_before_old(1)


    lane = lax.broadcasted_iota(jnp.int32, (16, 2 * C), 1)

    def spread_fine(f, fn):
        top = jnp.where(first_h, 0.0, fn(lt[1, f, 9].astype(F32)))
        bottom = jnp.where(last_h, 0.0, fn(lt[0, f, 9].astype(F32)))
        for p in range(9):
            even = fn(lt[0, f, p].astype(F32))
            odd = fn(lt[1, f, p].astype(F32))
            before = jnp.where(row16w == 0, top[p : p + 1], rolled(odd, 1))
            after = jnp.where(row16w == 15, bottom[p : p + 1], rolled(even, -1))
            for k, part in enumerate((before, even, odd, after)):
                if p == 0:
                    part = jnp.where(first_w & (lane < C), 0.0, part)
                if p == 8:
                    part = jnp.where(last_w & (lane >= C), 0.0, part)
                part = part.astype(BF16)
                for b in range(2):
                    lf[f, 2 * p + b, :, k * C : (k + 1) * C] = part[:, b * C : (b + 1) * C]

    @pl.when(ta == 0)
    def _():
        for copy in cf_second:
            copy.wait_recv()

    _, mean, half_scale, half_shift = normaliser(1, affine[2], affine[3])
    mean2 = jnp.concatenate([mean, mean], axis=1)
    scale2 = jnp.concatenate([half_scale, half_scale], axis=1)
    shift2 = jnp.concatenate([half_shift, half_shift], axis=1)

    def fine_act(x):
        half = (x - mean2) * scale2 + shift2
        return half + half * jnp.tanh(half)

    def fine_act_or_cached(x):
        return jnp.where(ta == 0, x, fine_act(x))

    def conv_fine(g):
        lhs = jnp.concatenate([lf[g, dw : dw + 16] for dw in range(3)], axis=-1).reshape(16 * 16, 12 * C)
        for f in range(2):
            dt = g - f
            if 0 <= dt <= 2:
                weights = w3[3 * dt : 3 * dt + 3].reshape(12 * C, 2 * C1)
                acc3[f] += jnp.dot(lhs, weights, preferred_element_type=F32).reshape(8, 2, 16, 2 * C1)

    def finish_fine(f):
        for c in range(16):
            for a in range(2):
                back[pl.ds(f * 512 + a * 16 + c, 16, stride=32), :] = acc3[f, c // 2, c % 2, :, a * C1 : (a + 1) * C1]
        out_ref[f * 512 : (f + 1) * 512] = back[f * 512 : (f + 1) * 512].astype(BF16)

    spread_fine(0, fine_act_or_cached)
    for g in range(4):
        if g < 3:
            spread_fine(g + 1, fine_act_or_cached if g + 1 < 2 else fine_act)
        conv_fine(g)
        if g >= 2:
            finish_fine(g - 2)

    for which in range(2):
        for stage in range(3):
            for copy in ar_copies(which, stage):
                copy.wait_send()
    for copy in first + second:
        copy.wait_send()

    @pl.when(ta < 2)
    def _():
        for copy in cm_first + cm_second:
            copy.wait_send()

    @pl.when(ta == 0)
    def _():
        for copy in cf_first + cf_second:
            copy.wait_send()

    @pl.when(ta < nt - 1)
    def _():
        for copy in to_next:
            copy.wait_send()

    @pl.when(jnp.logical_or(ta == 0, ta == 2))
    def _():
        to_second.wait_send()


def local(
    sizes, coarse, cache_coarse, cache_middle, cache_fine, coarse_gain, coarse_shift, fine_gain, fine_shift,
    coarse_kernel, lift_kernel, fine_kernel, skip_kernel,
):
    nt, nh, nw, C, C1 = sizes
    frames, rows, cols, _ = coarse.shape
    assert (frames, rows, cols) == (2, 16, 8)
    peers = nw + nh + nt - 3
    hbm = pl.BlockSpec(memory_space=pltpu.HBM)
    vmem = pl.BlockSpec(memory_space=pltpu.VMEM)
    V = pltpu.VMEM
    W = min(128, C)
    L = C // W
    scratch = [
        V((4, 1, C), F32),
        V((256, C), BF16), V((256, C), BF16), V((256, C), BF16), V((1024, C), BF16),
        V((L, 256, W), F32), V((L, 1024, W), F32),
        V((4, 12, 16, C), BF16), V((2, 8, 16, C), BF16), V((L, 4 * 12 * 16 + 64, W), F32),
        V((2, 4, 2, 16, C), BF16), V((2, 4, 2, 16, C), BF16), V((4, 2, 2, 16, C), F32),
        V((4, 18, 16, 3 * C), BF16), V((2, 12, 16, C), F32),
        V((3, 9 * C, C), BF16), V((3, 3, 3, C, C), BF16), V((2, 3, 4 * C, 2 * C), BF16),
        V((9, 4 * C, 2 * C1), BF16), V((2 * C, 2 * C1), BF16),
        V((2, 12, 16, C), BF16), V((2, 2, 16, C), BF16), V((2, 2, 1, 16, 2 * C), BF16),
        V((6, 12, 16, C), BF16), V((6, 14, 16, 3 * C), BF16), V((2 * L, 256, W), F32),
        V((2, 2, 10, 16, 2 * C), F32), V((2, 4, 10, 16, 2 * C), BF16),
        V((4, 18, 16, 4 * C), BF16), V((2, 8, 2, 16, 2 * C1), F32), V((1024, C1), F32),
        V((2, 3, 8, C), F32), V((2, peers, 8, C), F32),
        pltpu.SemaphoreType.DMA((60,)),
        pltpu.SemaphoreType.DMA((2, peers)), pltpu.SemaphoreType.DMA((2, peers)),
        pltpu.SemaphoreType.DMA((18,)), pltpu.SemaphoreType.DMA((18,)),
    ]
    decoded = pl.pallas_call(
        functools.partial(body, sizes),
        out_shape=jax.ShapeDtypeStruct((1024, C1), BF16),
        in_specs=[hbm] * 12,
        out_specs=vmem,
        scratch_shapes=scratch,
        compiler_params=pltpu.CompilerParams(
            collective_id=0, has_side_effects=True, vmem_limit_bytes=63 * 1024 * 1024
        ),
    )(
        coarse.reshape(256, C), cache_coarse.reshape(256, C), cache_middle.reshape(256, C), cache_fine.reshape(1024, C),
        coarse_gain.reshape(1, C), coarse_shift.reshape(1, C), fine_gain.reshape(1, C), fine_shift.reshape(1, C),
        coarse_kernel, lift_kernel, fine_kernel, skip_kernel,
    )
    return decoded.reshape(2, 32, 16, C1)


def solution(mesh):
    def run(*args):
        channels, outer = args[-1].shape
        sizes = (mesh.shape["ta"], mesh.shape["ha"], mesh.shape["wa"], channels, outer)
        return jax.shard_map(
            functools.partial(local, sizes),
            mesh=mesh,
            in_specs=(P("ta", "ha", "wa", None),) + (P(None, "ha", "wa", None),) * 3 + (P(),) * 8,
            out_specs=P("ta", "ha", "wa", None),
            check_vma=False,
        )(*args)

    return run
```

time: 426 us -> 51.4 us (0.12); the launches traced: 420 us -> 51.3 us
  blocking collectives: 311 us -> 0 us
  Pallas kernels: 0 us -> 49.6 us
  starting transfers between devices: 39.2 us -> 0 us
  waiting for transfers between devices: 29.4 us -> 0 us
  matrix products: 14 us -> 0 us
  local copies, waits for them, and re-layouts: 15.6 us -> 1.67 us
  other arithmetic: 10.1 us -> 0 us
    psum x4 -> x0, blocking collectives: 311 us -> none  [the longest x2 164 us: norm_act(): totals = lax.psum(jnp.sum(floats, axis=(0, 1, 2)), ('ta', 'ha', 'wa'))]
    pallas_call x0 -> x1, Pallas kernels: none -> 49.6 us  [local(): pl.pallas_call(functools.partial(body, sizes), out_shape=jax.ShapeDtypeSt...]
    ppermute x15 -> x0, starting transfers between devices: 39.2 us -> none  [the longest x3 15.6 us: from_behind(): lax.ppermute(value, axis, [(source, source + steps) for source in range(i...]
    ppermute x15 -> x0, waiting for transfers between devices: 29.4 us -> none  [the longest x6 15.5 us: padded_2(): after = lax.ppermute(initial, axis, down)]
    dot_general x28 -> x0, matrix products: 14 us -> none  [the longest x27 13 us: conv_taps(): jnp.dot(window.reshape(-1, 3 * inner), weights, preferred_element_type=jn...]
    slice x17 -> x0, local copies, waits for them, and re-layouts: 8.86 us -> none  [the longest x3 5.76 us: conv_taps(): weights = kernel[depth_tap, row_tap].reshape(3 * inner, outer)]
    concatenate x27 -> x0, other arithmetic: 5.36 us -> none  [the longest x6 3.09 us: padded_2(): shard = jnp.concatenate([before, shard, after], axis=dim)]
  transfers between devices with their start and end apart: 15 -> 0, of which waited for: 9 -> 0; matrix products, arithmetic and copies ran while one was open for 2% -> 0% of each run, Pallas kernels for 0% -> 0%
where the time goes in v1:
time: 51.4 us; the launch traced here: 51.3 us
  Pallas kernels  49.6 us (96%)
  local copies, waits for them, and re-layouts  1.67 us (3%)
    pallas_call x1, Pallas kernels, local(): pl.pallas_call(functools.partial(body, sizes), out_shape=jax.ShapeDtypeSt...  49.6 us
    unnamed x1, local copies, waits for them, and re-layouts  1.67 us

profile of v1, /device:TPU:1, one launch (start us, length us, event | category | flops | bytes accessed | tf_op | source)
XLA Modules:
  0.0 51.3 jit_solution(9080049406539465551)
XLA Ops:
  0.0 49.6 %shard_map.118 = bf16[1024,128]{1,0:T(8,128)(2,1)} custom-call(bf16[256,256]{1,0:T(8,128)(2,1)} %bitcast.11, bf16[256,256]{1,0:T(8,128)(2,1)} %bitcast.12, bf16[256,256]{1,0:T(8,128)(2,1)} %bitcast.13, bf16[1024,256]{1,0:T(8,128)(2,1)} %bitcast.10, f32[1,256]{1,0:T(1,128)} %bitcast.14, f32[1,256]{1,0:T(1,128)} %bitcast.15, f32[1,256]{1,0:T(1,128)} %bitcast.16, ...), custom_call_target="tpu_custom_call" | custom-call | tf_op jit(solution)/shard_map/pallas_call | solution.py:644
  49.6 1.7 %copy.14 = bf16[2,32,16,128]{3,2,1,0:T(8,128)(2,1)} copy(bf16[2,32,16,128]{3,2,1,0:T(8,128)(2,1)} %bitcast.9) | data formatting | bytes 524288

commit v2 on v1

--- a/solution.py
+++ b/solution.py
@@ -37,8 +37,8 @@
     coarse_gain, coarse_shift, fine_gain, fine_shift,
     coarse_kernel, lift_kernel, fine_kernel, skip_kernel,
     out_ref, affine,
-    cb, ccb, cmb, cfb, xf, cff, xt, ts, xtf, ss, sr, saf, act_a, acc1, w1, lk, w2, w3, skw,
-    cm, cs, cfs, mt, mid_g, gf, acc2, lt, lf, acc3, back, ar_src, ar_recv,
+    cb, cbp, cmb, cfb, xf, cff, xt, xtf, ss, sr, saf, act_a, acc1, w1, lk, w2, w3, skw,
+    cm, cs, cfs, mt, mid_g, gf, acc2, lt, lf, acc3, back, outb, ar_src, ar_recv,
     local_sem, ar_send, ar_got, send_sem, recv_sem,
 ):
     nt, nh, nw, C, C1 = sizes
@@ -68,11 +68,25 @@
 
     get_coarse = load(coarse_hbm, cb)
     barrier = pltpu.get_barrier_semaphore()
-    friends = [near(w=d) for d in range(1, nw)] + [near(h=d) for d in range(1, nh)] + [near(t=d) for d in range(1, nt)]
-    friends += [near(t=-1, w=1), near(t=-1, w=-1)]
+    y_hi, core = ta // 2, lax.rem(ta, 2)
+    by_z = [
+        {"ta": 2 * y_hi + lax.rem(core + dc, 2), "ha": lax.rem(ha + dh, nh)}
+        for dc in range(2) for dh in range(nh) if dc or dh
+    ]
+    by_xy = [
+        {"ta": 2 * lax.rem(y_hi + dy, 2) + core, "wa": lax.rem(wa + dw, nw)}
+        for dy in range(2) for dw in range(nw) if dy or dw
+    ]
+    stages = ((by_z, 0), (by_xy, len(by_z)))
+    friends = by_z + by_xy + [near(t=-1), near(t=-1, w=1), near(t=-1, w=-1), near(t=-1, h=1), near(t=-1, h=-1)]
     for friend in friends:
         pl.semaphore_signal(barrier, inc=1, device_id=friend, device_id_type=MESH)
-    get_cc = load(cache_coarse_hbm, ccb)
+    get_cc = pltpu.make_async_copy(cache_coarse_hbm, cbp, local_sem.at[59])
+
+    @pl.when(ta == 0)
+    def _():
+        get_cc.start()
+
     get_cm = load(cache_middle_hbm, cmb)
     get_cf = load(cache_fine_hbm, cfb)
     get_lk = load(lift_kernel, lk)
@@ -87,35 +101,79 @@
     get_affine = [load(ref, affine.at[i]) for i, ref in enumerate((coarse_gain, coarse_shift, fine_gain, fine_shift))]
     get_skip = [load(skip_kernel, skw.at[a * C : (a + 1) * C, a * C1 : (a + 1) * C1]) for a in range(2)]
 
+    def message(index, src, dst, where, leaves=None):
+        return pltpu.make_async_remote_copy(
+            src_ref=src, dst_ref=dst, send_sem=send_sem.at[index if leaves is None else leaves], recv_sem=recv_sem.at[index],
+            device_id=where, device_id_type=MESH,
+        )
+
+    center = message(0, coarse_hbm, cbp, near(t=1))
+    cols_own = [
+        message(1, xt.at[2:4, 8:10], xt.at[2:4, 0:2], near(w=1)),
+        message(2, xt.at[2:4, 2:4], xt.at[2:4, 10:12], near(w=-1)),
+    ]
+    cols_next = [
+        message(3, xt.at[2:4, 8:10], xt.at[0:2, 0:2], near(t=1, w=1)),
+        message(4, xt.at[2:4, 2:4], xt.at[0:2, 10:12], near(t=1, w=-1)),
+    ]
+    cols_cached = [
+        message(3, xt.at[0:2, 8:10], xt.at[0:2, 0:2], near(w=1), 18),
+        message(4, xt.at[0:2, 2:4], xt.at[0:2, 10:12], near(w=-1), 19),
+    ]
+    rows_own = [
+        message(9, ss.at[0, 2:4], sr.at[1, 2:4], near(h=-1)),
+        message(10, ss.at[1, 2:4], sr.at[0, 2:4], near(h=1)),
+    ]
+    rows_next = [
+        message(20, ss.at[0, 2:4], sr.at[1, 0:2], near(t=1, h=-1)),
+        message(21, ss.at[1, 2:4], sr.at[0, 0:2], near(t=1, h=1)),
+    ]
+    rows_cached = [
+        message(20, ss.at[0, 0:2], sr.at[1, 0:2], near(h=-1), 22),
+        message(21, ss.at[1, 0:2], sr.at[0, 0:2], near(h=1), 23),
+    ]
+
+    pl.semaphore_wait(barrier, len(friends))
+
+    @pl.when(ta < nt - 1)
+    def _():
+        center.start()
+
+    def transpose_into(first_frame):
+        for f in range(2):
+            for c in range(8):
+                cells = take(xf, f * 128 + c, 8)
+                put(xtf, (first_frame + f) * 192 + (2 + c) * 16, cells)
+                xt[first_frame + f, 2 + c] = cells.astype(BF16)
+
     get_coarse.wait()
     flat = cb[...].astype(F32)
     put(xf, 0, flat)
+    transpose_into(2)
+    for copy in cols_own:
+        copy.start()
+
+    @pl.when(ta < nt - 1)
+    def _():
+        for copy in cols_next:
+            copy.start()
+
     count = flat.shape[0]
     mean = jnp.sum(flat, axis=0, keepdims=True) / count
     centred = flat - mean
     ar_src[0, 0] = jnp.zeros((8, C), F32)
     ar_src[0, 0, 0:1, :] = mean
     ar_src[0, 0, 1:2, :] = jnp.sum(centred * centred, axis=0, keepdims=True) / count
-    get_cc.wait()
-    pl.semaphore_wait(barrier, len(friends))
-
-    def message(index, src, dst, where):
-        return pltpu.make_async_remote_copy(
-            src_ref=src, dst_ref=dst, send_sem=send_sem.at[index], recv_sem=recv_sem.at[index],
-            device_id=where, device_id_type=MESH,
-        )
-
-    stages = ((("w", nw), 0), (("h", nh), nw - 1), (("t", nt), nw - 1 + nh - 1))
 
     def ar_copies(which, stage):
-        (axis, n), base = stages[stage]
+        peers, base = stages[stage]
         return [
             pltpu.make_async_remote_copy(
-                src_ref=ar_src.at[which, stage], dst_ref=ar_recv.at[which, base + d - 1],
-                send_sem=ar_send.at[which, base + d - 1], recv_sem=ar_got.at[which, base + d - 1],
-                device_id=near(**{axis: d}), device_id_type=MESH,
+                src_ref=ar_src.at[which, stage], dst_ref=ar_recv.at[which, base + i],
+                send_sem=ar_send.at[which, base + i], recv_sem=ar_got.at[which, base + i],
+                device_id=peer, device_id_type=MESH,
             )
-            for d in range(1, n)
+            for i, peer in enumerate(peers)
         ]
 
     def ar_start(which, stage):
@@ -123,10 +181,11 @@
             copy.start()
 
     def ar_finish(which, stage):
-        (_, n), base = stages[stage]
+        peers, base = stages[stage]
+        n = len(peers) + 1
         for copy in ar_copies(which, stage):
             copy.wait_recv()
-        tiles = [ar_src[which, stage]] + [ar_recv[which, base + d - 1] for d in range(1, n)]
+        tiles = [ar_src[which, stage]] + [ar_recv[which, base + i] for i in range(n - 1)]
         average = functools.reduce(jnp.add, tiles) / n
         spread = functools.reduce(jnp.add, [(tile - average) * (tile - average) for tile in tiles]) / n
         rows = lax.broadcasted_iota(jnp.int32, (8, C), 0)
@@ -152,7 +211,7 @@
         return jnp.concatenate(parts, axis=1) / size
 
     def normaliser(which, gain, shift):
-        tile = ar_finish(which, 2)
+        tile = ar_finish(which, 1)
         mean, variance = tile[0:1], tile[1:2]
         grouped = group_mean(mean)
         away = mean - grouped
@@ -167,30 +226,14 @@
         return act, mean, half_scale, half_shift
 
     ar_start(0, 0)
-    for f in range(2):
-        for c in range(8):
-            xt[2 + f, 2 + c] = take(xf, f * 128 + c, 8).astype(BF16)
-
-    @pl.when(ta == nt - 1)
-    def _():
-        put(xf, 0, ccb[...].astype(F32))
-        for f in range(2):
-            for c in range(8):
-                ts[f, c] = take(xf, f * 128 + c, 8).astype(BF16)
-
-    @pl.when(ta != nt - 1)
-    def _():
-        ts[...] = xt[2:4, 2:10]
-
-    first = [
-        message(0, ts, xt.at[0:2, 2:10], near(t=1)),
-        message(1, xt.at[2:4, 8:10], xt.at[2:4, 0:2], near(w=1)),
-        message(2, xt.at[2:4, 2:4], xt.at[2:4, 10:12], near(w=-1)),
-        message(3, ts.at[:, 6:8], xt.at[0:2, 0:2], near(t=1, w=1)),
-        message(4, ts.at[:, 0:2], xt.at[0:2, 10:12], near(t=1, w=-1)),
-    ]
-    for copy in first:
-        copy.start()
+
+    @pl.when(ta == 0)
+    def _():
+        get_cc.wait()
+        put(xf, 0, cbp[...].astype(F32))
+        transpose_into(0)
+        for copy in cols_cached:
+            copy.start()
 
     cm_first = [
         message(5, cm.at[:, 8:9], cm.at[:, 0:1], near(w=1)),
@@ -226,6 +269,38 @@
             w3[3 * dt + dw, 0:C, C1 : 2 * C1] = jnp.zeros((C, C1), BF16)
     skw[0:C, C1 : 2 * C1] = jnp.zeros((C, C1), BF16)
     skw[C : 2 * C, 0:C1] = jnp.zeros((C, C1), BF16)
+    def widen(f, slots):
+        for c in slots:
+            put(xtf, f * 192 + c * 16, xt[f, c].astype(F32))
+
+    def pick_rows(f):
+        for side, rows in enumerate(((0, 1), (14, 15))):
+            for k, row in enumerate(rows):
+                ss[side, f, k] = take(xtf, f * 192 + row, 16).astype(BF16)
+
+    for copy in cols_own:
+        copy.wait_recv()
+    for f in (2, 3):
+        widen(f, (0, 1, 10, 11))
+        pick_rows(f)
+    for copy in rows_own:
+        copy.start()
+
+    @pl.when(ta < nt - 1)
+    def _():
+        for copy in rows_next:
+            copy.start()
+
+    @pl.when(ta == 0)
+    def _():
+        for copy in cols_cached:
+            copy.wait_recv()
+        for f in (0, 1):
+            widen(f, (0, 1, 10, 11))
+            pick_rows(f)
+        for copy in rows_cached:
+            copy.start()
+
     def fold(i, carry):
         dt, r = i // (C // 16), pl.multiple_of(lax.rem(i, C // 16) * 16, 16)
         taps = [[lk[dt, dh, dw, pl.ds(r, 16), :].astype(F32) for dw in range(3)] for dh in range(3)]
@@ -244,28 +319,6 @@
     get_lk.wait()
     ar_next(0, 0)
     lax.fori_loop(0, 3 * (C // 32), fold, 0)
-    ar_next(0, 1)
-
-    for copy in first:
-        copy.wait_recv()
-
-    def widen(i, carry):
-        f, c = i // 12, i % 12
-        put(xtf, pl.multiple_of(i * 16, 16), xt[f, c].astype(F32))
-        return carry
-
-    lax.fori_loop(0, 48, widen, 0, unroll=8)
-    for f in range(4):
-        for side, rows in enumerate(((0, 1), (14, 15))):
-            for k, row in enumerate(rows):
-                ss[side, f, k] = take(xtf, f * 192 + row, 16).astype(BF16)
-    second = [
-        message(9, ss.at[0], sr.at[1], near(h=-1)),
-        message(10, ss.at[1], sr.at[0], near(h=1)),
-    ]
-    for copy in second:
-        copy.start()
-
     @pl.when(ta < 2)
     def _():
         for copy in cm_first:
@@ -278,11 +331,23 @@
         for copy in cm_second:
             copy.start()
 
+    @pl.when(ta > 0)
+    def _():
+        center.wait_recv()
+        put(xf, 0, cbp[...].astype(F32))
+        for f in range(2):
+            for c in range(8):
+                put(xtf, f * 192 + (2 + c) * 16, take(xf, f * 128 + c, 8))
+        for copy in cols_next:
+            copy.wait_recv()
+        for f in (0, 1):
+            widen(f, (0, 1, 10, 11))
+
     lax.fori_loop(3 * (C // 32), 3 * (C // 16), fold, 0)
     for copy in get_w1 + get_w3 + get_skip + get_affine:
         copy.wait()
 
-    for copy in second:
+    for copy in rows_own + rows_next:
         copy.wait_recv()
     act, *_ = normaliser(0, affine[0], affine[1])
 
@@ -321,7 +386,7 @@
                 for dh in range(3):
                     act_a[f, 12 + 2 * dw + side, :, dh * C : (dh + 1) * C] = rolled(lines[dh], -dw).astype(BF16)
 
-    def conv_coarse(g):
+    def conv_coarse(f, g):
         lhs = jnp.concatenate(
             [
                 jnp.concatenate([act_a[g, dw : dw + 10], act_a[g, 12 + 2 * dw : 14 + 2 * dw]], axis=0)
@@ -329,10 +394,8 @@
             ],
             axis=-1,
         ).reshape(12 * 16, 9 * C)
-        for f in range(2):
-            if 0 <= g - f <= 2:
-                part = jnp.dot(lhs, w1[g - f], preferred_element_type=F32).reshape(12, 16, C)
-                acc1[f] = part if g == f else acc1[f] + part
+        part = jnp.dot(lhs, w1[g - f], preferred_element_type=F32).reshape(12, 16, C)
+        acc1[f] = part if g == f else acc1[f] + part
 
     def finish_middle(f):
         for c in range(10):
@@ -358,12 +421,16 @@
             to_next[f].start()
 
     act_coarse(0)
-    for g in range(4):
-        if g < 3:
-            act_coarse(g + 1)
-        conv_coarse(g)
-        if g >= 2:
-            send_middle(g - 2)
+    act_coarse(1)
+    conv_coarse(0, 0)
+    act_coarse(2)
+    conv_coarse(0, 1)
+    conv_coarse(0, 2)
+    send_middle(0)
+    act_coarse(3)
+    for g in (1, 2, 3):
+        conv_coarse(1, g)
+    send_middle(1)
 
     to_second = message(17, mt.at[4:6], mt.at[0:2], near(t=2))
     by_second = message(17, mt.at[2:4], mt.at[0:2], near(t=1))
@@ -442,21 +509,22 @@
     def _():
         to_second.start()
 
-    def own_sums(fn):
-        total = jnp.zeros((16, C), F32)
-        for a in range(2):
-            for f in range(2):
-                for p in range(9):
-                    for b in range(2):
-                        if (p, b) in ((0, 0), (8, 1)):
-                            continue
-                        total = total + fn(lt[a, 2 + f, p, :, b * C : (b + 1) * C].astype(F32))
-        return jnp.sum(total, axis=0, keepdims=True) / (2 * 2 * 16 * 16)
-
-    mean = own_sums(lambda x: x)
+    pivot = jnp.sum(lt[0, 2, 1, :, 0:C].astype(F32), axis=0, keepdims=True) / 16
+    sums = jnp.zeros((16, C), F32)
+    squares = jnp.zeros((16, C), F32)
+    for a in range(2):
+        for f in range(2):
+            for p in range(9):
+                for b in range(2):
+                    if (p, b) not in ((0, 0), (8, 1)):
+                        x = lt[a, 2 + f, p, :, b * C : (b + 1) * C].astype(F32) - pivot
+                        sums = sums + x
+                        squares = squares + x * x
+    count = 2 * 2 * 16 * 16
+    off = jnp.sum(sums, axis=0, keepdims=True) / count
     ar_src[1, 0] = jnp.zeros((8, C), F32)
-    ar_src[1, 0, 0:1, :] = mean
-    ar_src[1, 0, 1:2, :] = own_sums(lambda x: (x - mean) * (x - mean))
+    ar_src[1, 0, 0:1, :] = pivot + off
+    ar_src[1, 0, 1:2, :] = jnp.maximum(jnp.sum(squares, axis=0, keepdims=True) / count - off * off, 0.0)
     ar_start(1, 0)
 
     def lift_before_new(a):
@@ -504,8 +572,6 @@
         lhs = jnp.concatenate([lt[a, 2:4, 1 - b : 9 - b, :, b * C : (b + 1) * C] for a in range(2)], axis=-1)
         part = jnp.dot(lhs.reshape(2 * 8 * 16, 2 * C), skw[...], preferred_element_type=F32)
         acc3[:, :, 1 - b] = part.reshape(2, 8, 16, 2 * C1)
-
-    ar_next(1, 1)
 
     @pl.when(ta == 1)
     def _():
@@ -573,7 +639,13 @@
         for c in range(16):
             for a in range(2):
                 back[pl.ds(f * 512 + a * 16 + c, 16, stride=32), :] = acc3[f, c // 2, c % 2, :, a * C1 : (a + 1) * C1]
-        out_ref[f * 512 : (f + 1) * 512] = back[f * 512 : (f + 1) * 512].astype(BF16)
+        outb[f * 512 : (f + 1) * 512] = back[f * 512 : (f + 1) * 512].astype(BF16)
+        leave[f].start()
+
+    leave = [
+        pltpu.make_async_copy(outb.at[f * 512 : (f + 1) * 512], out_ref.at[f * 512 : (f + 1) * 512], local_sem.at[57 + f])
+        for f in range(2)
+    ]
 
     spread_fine(0, fine_act_or_cached)
     for g in range(4):
@@ -583,11 +655,13 @@
         if g >= 2:
             finish_fine(g - 2)
 
+    for copy in leave:
+        copy.wait()
     for which in range(2):
-        for stage in range(3):
+        for stage in range(2):
             for copy in ar_copies(which, stage):
                 copy.wait_send()
-    for copy in first + second:
+    for copy in cols_own + rows_own:
         copy.wait_send()
 
     @pl.when(ta < 2)
@@ -597,12 +671,12 @@
 
     @pl.when(ta == 0)
     def _():
-        for copy in cf_first + cf_second:
+        for copy in cols_cached + rows_cached + cf_first + cf_second:
             copy.wait_send()
 
     @pl.when(ta < nt - 1)
     def _():
-        for copy in to_next:
+        for copy in [center] + cols_next + rows_next + to_next:
             copy.wait_send()
 
     @pl.when(jnp.logical_or(ta == 0, ta == 2))
@@ -617,9 +691,8 @@
     nt, nh, nw, C, C1 = sizes
     frames, rows, cols, _ = coarse.shape
     assert (frames, rows, cols) == (2, 16, 8)
-    peers = nw + nh + nt - 3
+    peers = 2 * nh + 2 * nw - 2
     hbm = pl.BlockSpec(memory_space=pltpu.HBM)
-    vmem = pl.BlockSpec(memory_space=pltpu.VMEM)
     V = pltpu.VMEM
     W = min(128, C)
     L = C // W
@@ -627,7 +700,7 @@
         V((4, 1, C), F32),
         V((256, C), BF16), V((256, C), BF16), V((256, C), BF16), V((1024, C), BF16),
         V((L, 256, W), F32), V((L, 1024, W), F32),
-        V((4, 12, 16, C), BF16), V((2, 8, 16, C), BF16), V((L, 4 * 12 * 16 + 64, W), F32),
+        V((4, 12, 16, C), BF16), V((L, 4 * 12 * 16 + 64, W), F32),
         V((2, 4, 2, 16, C), BF16), V((2, 4, 2, 16, C), BF16), V((4, 2, 2, 16, C), F32),
         V((4, 18, 16, 3 * C), BF16), V((2, 12, 16, C), F32),
         V((3, 9 * C, C), BF16), V((3, 3, 3, C, C), BF16), V((2, 3, 4 * C, 2 * C), BF16),
@@ -635,17 +708,17 @@
         V((2, 12, 16, C), BF16), V((2, 2, 16, C), BF16), V((2, 2, 1, 16, 2 * C), BF16),
         V((6, 12, 16, C), BF16), V((6, 14, 16, 3 * C), BF16), V((2 * L, 256, W), F32),
         V((2, 2, 10, 16, 2 * C), F32), V((2, 4, 10, 16, 2 * C), BF16),
-        V((4, 18, 16, 4 * C), BF16), V((2, 8, 2, 16, 2 * C1), F32), V((1024, C1), F32),
-        V((2, 3, 8, C), F32), V((2, peers, 8, C), F32),
+        V((4, 18, 16, 4 * C), BF16), V((2, 8, 2, 16, 2 * C1), F32), V((1024, C1), F32), V((1024, C1), BF16),
+        V((2, 2, 8, C), F32), V((2, peers, 8, C), F32),
         pltpu.SemaphoreType.DMA((60,)),
         pltpu.SemaphoreType.DMA((2, peers)), pltpu.SemaphoreType.DMA((2, peers)),
-        pltpu.SemaphoreType.DMA((18,)), pltpu.SemaphoreType.DMA((18,)),
+        pltpu.SemaphoreType.DMA((24,)), pltpu.SemaphoreType.DMA((24,)),
     ]
     decoded = pl.pallas_call(
         functools.partial(body, sizes),
         out_shape=jax.ShapeDtypeStruct((1024, C1), BF16),
         in_specs=[hbm] * 12,
-        out_specs=vmem,
+        out_specs=hbm,
         scratch_shapes=scratch,
         compiler_params=pltpu.CompilerParams(
             collective_id=0, has_side_effects=True, vmem_limit_bytes=63 * 1024 * 1024

time: 51.4 us -> 49 us (0.953)
  Pallas kernels: 49.6 us -> 47.2 us
    pallas_call x1, Pallas kernels: 49.6 us -> 47.2 us  [local(): pl.pallas_call(functools.partial(body, sizes), out_shape=jax.ShapeDtypeSt...]
where the time goes in v2:
time: 49 us; the launch traced here: 48.9 us
  Pallas kernels  47.2 us (96%)
  local copies, waits for them, and re-layouts  1.67 us (3%)
    pallas_call x1, Pallas kernels, local(): pl.pallas_call(functools.partial(body, sizes), out_shape=jax.ShapeDtypeSt...  47.2 us
    unnamed x1, local copies, waits for them, and re-layouts  1.67 us

profile of v2, /device:TPU:1, one launch (start us, length us, event | category | flops | bytes accessed | tf_op | source)
XLA Modules:
  0.0 48.9 jit_solution(11612266450380974802)
XLA Ops:
  0.0 47.2 %shard_map.118 = bf16[1024,128]{1,0:T(8,128)(2,1)} custom-call(bf16[256,256]{1,0:T(8,128)(2,1)} %bitcast.11, bf16[256,256]{1,0:T(8,128)(2,1)} %bitcast.12, bf16[256,256]{1,0:T(8,128)(2,1)} %bitcast.13, bf16[1024,256]{1,0:T(8,128)(2,1)} %bitcast.10, f32[1,256]{1,0:T(1,128)} %bitcast.14, f32[1,256]{1,0:T(1,128)} %bitcast.15, f32[1,256]{1,0:T(1,128)} %bitcast.16, ...), custom_call_target="tpu_custom_call" | custom-call | tf_op jit(solution)/shard_map/pallas_call | solution.py:717
  47.2 1.7 %copy.14 = bf16[2,32,16,128]{3,2,1,0:T(8,128)(2,1)} copy(bf16[2,32,16,128]{3,2,1,0:T(8,128)(2,1)} %bitcast.9) | data formatting | bytes 524288

commit v3 on v2

--- a/solution.py
+++ b/solution.py
@@ -87,19 +87,7 @@
     def _():
         get_cc.start()
 
-    get_cm = load(cache_middle_hbm, cmb)
-    get_cf = load(cache_fine_hbm, cfb)
     get_lk = load(lift_kernel, lk)
-    get_w1 = [
-        load(coarse_kernel.at[dt, dh, dw], w1.at[dt, (3 * dw + dh) * C : (3 * dw + dh + 1) * C])
-        for dt in range(3) for dh in range(3) for dw in range(3)
-    ]
-    get_w3 = [
-        load(fine_kernel.at[dt, dh], w3.at[3 * dt : 3 * dt + 3, (a + dh) * C : (a + dh + 1) * C, a * C1 : (a + 1) * C1])
-        for dt in range(3) for dh in range(3) for a in range(2)
-    ]
-    get_affine = [load(ref, affine.at[i]) for i, ref in enumerate((coarse_gain, coarse_shift, fine_gain, fine_shift))]
-    get_skip = [load(skip_kernel, skw.at[a * C : (a + 1) * C, a * C1 : (a + 1) * C1]) for a in range(2)]
 
     def message(index, src, dst, where, leaves=None):
         return pltpu.make_async_remote_copy(
@@ -226,6 +214,12 @@
         return act, mean, half_scale, half_shift
 
     ar_start(0, 0)
+    get_cm = load(cache_middle_hbm, cmb)
+    get_w1 = load(coarse_kernel, w1)
+    get_affine = [load(ref, affine.at[i]) for i, ref in enumerate((coarse_gain, coarse_shift, fine_gain, fine_shift))]
+    get_w3 = [load(fine_kernel, w3.at[:, a : a + 3, :, :, a * C1 : (a + 1) * C1]) for a in range(2)]
+    get_skip = [load(skip_kernel, skw.at[a * C : (a + 1) * C, a * C1 : (a + 1) * C1]) for a in range(2)]
+    get_cf = load(cache_fine_hbm, cfb)
 
     @pl.when(ta == 0)
     def _():
@@ -265,8 +259,8 @@
 
     for dt in range(3):
         for dw in range(3):
-            w3[3 * dt + dw, 3 * C : 4 * C, 0:C1] = jnp.zeros((C, C1), BF16)
-            w3[3 * dt + dw, 0:C, C1 : 2 * C1] = jnp.zeros((C, C1), BF16)
+            w3[dt, 3, dw, :, 0:C1] = jnp.zeros((C, C1), BF16)
+            w3[dt, 0, dw, :, C1 : 2 * C1] = jnp.zeros((C, C1), BF16)
     skw[0:C, C1 : 2 * C1] = jnp.zeros((C, C1), BF16)
     skw[C : 2 * C, 0:C1] = jnp.zeros((C, C1), BF16)
     def widen(f, slots):
@@ -344,7 +338,7 @@
             widen(f, (0, 1, 10, 11))
 
     lax.fori_loop(3 * (C // 32), 3 * (C // 16), fold, 0)
-    for copy in get_w1 + get_w3 + get_skip + get_affine:
+    for copy in [get_w1] + get_affine:
         copy.wait()
 
     for copy in rows_own + rows_next:
@@ -389,12 +383,13 @@
     def conv_coarse(f, g):
         lhs = jnp.concatenate(
             [
-                jnp.concatenate([act_a[g, dw : dw + 10], act_a[g, 12 + 2 * dw : 14 + 2 * dw]], axis=0)
+                jnp.concatenate([act_a[g, dw : dw + 10, :, lanes], act_a[g, 12 + 2 * dw : 14 + 2 * dw, :, lanes]], axis=0)
+                for lanes in (slice(0, C), slice(C, 2 * C), slice(2 * C, 3 * C))
                 for dw in range(3)
             ],
             axis=-1,
         ).reshape(12 * 16, 9 * C)
-        part = jnp.dot(lhs, w1[g - f], preferred_element_type=F32).reshape(12, 16, C)
+        part = jnp.dot(lhs, w1[g - f].reshape(9 * C, C), preferred_element_type=F32).reshape(12, 16, C)
         acc1[f] = part if g == f else acc1[f] + part
 
     def finish_middle(f):
@@ -477,6 +472,8 @@
                 outside = jnp.logical_or(gone, first_h if side == 0 else last_h)
                 mt[at + f, 10 + side] = jnp.where(outside, 0.0, cm[f, 10 + side].astype(F32)).astype(BF16)
 
+    for copy in get_w3 + get_skip + [get_cf]:
+        copy.wait()
     prepare(4)
     prepare(5)
     for a in range(2):
@@ -488,6 +485,14 @@
         for copy in cm_second:
             copy.wait_recv()
         cached_middle(2)
+        put(cff, 0, cfb[...].astype(F32))
+        for f in range(2):
+            for c in range(16):
+                p, b = (c + 1) // 2, (c + 1) % 2
+                for a in range(2):
+                    lt[a, f, p, :, b * C : (b + 1) * C] = take(cff, f * 512 + a * 16 + c, 32).astype(BF16)
+        for copy in cf_first:
+            copy.start()
 
     @pl.when(ta > 0)
     def _():
@@ -529,32 +534,15 @@
 
     def lift_before_new(a):
         acc2[a] = lift_part(a, 2, 2, 2)
-        acc2[a, 1:2] += lift_part(a, 1, 2, 1)
 
     def lift_before_old(a):
         acc2[a] += lift_part(a, 0, 0, 2)
-        lt[a, 0:1] = (acc2[a, 0:1] + lift_part(a, 1, 1, 1)).astype(BF16)
-        lt[a, 1:2] = acc2[a, 1:2].astype(BF16)
+        lt[a, 0:2] = (acc2[a] + lift_part(a, 1, 1, 2)).astype(BF16)
 
     @pl.when(ta > 0)
     def _():
         lift_before_new(0)
         lift_before_new(1)
-
-    get_cf.wait()
-
-    @pl.when(ta == 0)
-    def _():
-        put(cff, 0, cfb[...].astype(F32))
-        for f in range(2):
-            for c in range(16):
-                p, b = (c + 1) // 2, (c + 1) % 2
-                for a in range(2):
-                    lt[a, f, p, :, b * C : (b + 1) * C] = take(cff, f * 512 + a * 16 + c, 32).astype(BF16)
-        for copy in cf_first:
-            copy.start()
-
-    ar_next(1, 0)
 
     @pl.when(ta == 0)
     def _():
@@ -567,6 +555,8 @@
                 cfs[a, f, 0] = take(gf, row, 16).astype(BF16)
         for copy in cf_second:
             copy.start()
+
+    ar_next(1, 0)
 
     for b in range(2):
         lhs = jnp.concatenate([lt[a, 2:4, 1 - b : 9 - b, :, b * C : (b + 1) * C] for a in range(2)], axis=-1)
@@ -627,13 +617,12 @@
     def fine_act_or_cached(x):
         return jnp.where(ta == 0, x, fine_act(x))
 
-    def conv_fine(g):
-        lhs = jnp.concatenate([lf[g, dw : dw + 16] for dw in range(3)], axis=-1).reshape(16 * 16, 12 * C)
-        for f in range(2):
-            dt = g - f
-            if 0 <= dt <= 2:
-                weights = w3[3 * dt : 3 * dt + 3].reshape(12 * C, 2 * C1)
-                acc3[f] += jnp.dot(lhs, weights, preferred_element_type=F32).reshape(8, 2, 16, 2 * C1)
+    def conv_fine(dt):
+        lhs = jnp.concatenate(
+            [lf[dt : dt + 2, dw : dw + 16, :, k * C : (k + 1) * C] for k in range(4) for dw in range(3)], axis=-1
+        ).reshape(2 * 16 * 16, 12 * C)
+        part = jnp.dot(lhs, w3[dt].reshape(12 * C, 2 * C1), preferred_element_type=F32)
+        acc3[...] += part.reshape(2, 8, 2, 16, 2 * C1)
 
     def finish_fine(f):
         for c in range(16):
@@ -648,12 +637,14 @@
     ]
 
     spread_fine(0, fine_act_or_cached)
-    for g in range(4):
-        if g < 3:
-            spread_fine(g + 1, fine_act_or_cached if g + 1 < 2 else fine_act)
-        conv_fine(g)
-        if g >= 2:
-            finish_fine(g - 2)
+    spread_fine(1, fine_act_or_cached)
+    spread_fine(2, fine_act)
+    conv_fine(0)
+    spread_fine(3, fine_act)
+    conv_fine(1)
+    conv_fine(2)
+    finish_fine(0)
+    finish_fine(1)
 
     for copy in leave:
         copy.wait()
@@ -703,8 +694,8 @@
         V((4, 12, 16, C), BF16), V((L, 4 * 12 * 16 + 64, W), F32),
         V((2, 4, 2, 16, C), BF16), V((2, 4, 2, 16, C), BF16), V((4, 2, 2, 16, C), F32),
         V((4, 18, 16, 3 * C), BF16), V((2, 12, 16, C), F32),
-        V((3, 9 * C, C), BF16), V((3, 3, 3, C, C), BF16), V((2, 3, 4 * C, 2 * C), BF16),
-        V((9, 4 * C, 2 * C1), BF16), V((2 * C, 2 * C1), BF16),
+        V((3, 3, 3, C, C), BF16), V((3, 3, 3, C, C), BF16), V((2, 3, 4 * C, 2 * C), BF16),
+        V((3, 4, 3, C, 2 * C1), BF16), V((2 * C, 2 * C1), BF16),
         V((2, 12, 16, C), BF16), V((2, 2, 16, C), BF16), V((2, 2, 1, 16, 2 * C), BF16),
         V((6, 12, 16, C), BF16), V((6, 14, 16, 3 * C), BF16), V((2 * L, 256, W), F32),
         V((2, 2, 10, 16, 2 * C), F32), V((2, 4, 10, 16, 2 * C), BF16),

time: 49 us -> 48.8 us (level)
  no operation moved by 1% of the time
where the time goes in v3:
time: 48.8 us; the launch traced here: 48.7 us
  Pallas kernels  47 us (96%)
  local copies, waits for them, and re-layouts  1.67 us (3%)
    pallas_call x1, Pallas kernels, local(): pl.pallas_call(functools.partial(body, sizes), out_shape=jax.ShapeDtypeSt...  47 us
    unnamed x1, local copies, waits for them, and re-layouts  1.67 us

profile of v3, /device:TPU:1, one launch (start us, length us, event | category | flops | bytes accessed | tf_op | source)
XLA Modules:
  0.0 48.7 jit_solution(13833734717574209053)
XLA Ops:
  0.0 47.0 %shard_map.118 = bf16[1024,128]{1,0:T(8,128)(2,1)} custom-call(bf16[256,256]{1,0:T(8,128)(2,1)} %bitcast.11, bf16[256,256]{1,0:T(8,128)(2,1)} %bitcast.12, bf16[256,256]{1,0:T(8,128)(2,1)} %bitcast.13, bf16[1024,256]{1,0:T(8,128)(2,1)} %bitcast.10, f32[1,256]{1,0:T(1,128)} %bitcast.14, f32[1,256]{1,0:T(1,128)} %bitcast.15, f32[1,256]{1,0:T(1,128)} %bitcast.16, ...), custom_call_target="tpu_custom_call" | custom-call | tf_op jit(solution)/shard_map/pallas_call | solution.py:708
  47.0 1.7 %copy.14 = bf16[2,32,16,128]{3,2,1,0:T(8,128)(2,1)} copy(bf16[2,32,16,128]{3,2,1,0:T(8,128)(2,1)} %bitcast.9) | data formatting | bytes 524288

commit v4 on v3

--- a/solution.py
+++ b/solution.py
@@ -37,7 +37,7 @@
     coarse_gain, coarse_shift, fine_gain, fine_shift,
     coarse_kernel, lift_kernel, fine_kernel, skip_kernel,
     out_ref, affine,
-    cb, cbp, cmb, cfb, xf, cff, xt, xtf, ss, sr, saf, act_a, acc1, w1, lk, w2, w3, skw,
+    cb, cbp, cmb, cfb, xf, cff, xt, xtf, ss, sr, saf, act_a, acc1, w1, lk, w2, w3, wp, skw,
     cm, cs, cfs, mt, mid_g, gf, acc2, lt, lf, acc3, back, outb, ar_src, ar_recv,
     local_sem, ar_send, ar_got, send_sem, recv_sem,
 ):
@@ -217,7 +217,11 @@
     get_cm = load(cache_middle_hbm, cmb)
     get_w1 = load(coarse_kernel, w1)
     get_affine = [load(ref, affine.at[i]) for i, ref in enumerate((coarse_gain, coarse_shift, fine_gain, fine_shift))]
-    get_w3 = [load(fine_kernel, w3.at[:, a : a + 3, :, :, a * C1 : (a + 1) * C1]) for a in range(2)]
+    get_w3 = [
+        load(fine_kernel.at[2 * i], w3.at[i, a : a + 3, :, :, a * C1 : (a + 1) * C1]) for i in range(2) for a in range(2)
+    ] + [
+        load(fine_kernel.at[1 + i - f], wp.at[i, :, :, :, f * C1 : (f + 1) * C1]) for i in range(2) for f in range(2)
+    ]
     get_skip = [load(skip_kernel, skw.at[a * C : (a + 1) * C, a * C1 : (a + 1) * C1]) for a in range(2)]
     get_cf = load(cache_fine_hbm, cfb)
 
@@ -257,12 +261,6 @@
         for copy in cm_first:
             copy.start()
 
-    for dt in range(3):
-        for dw in range(3):
-            w3[dt, 3, dw, :, 0:C1] = jnp.zeros((C, C1), BF16)
-            w3[dt, 0, dw, :, C1 : 2 * C1] = jnp.zeros((C, C1), BF16)
-    skw[0:C, C1 : 2 * C1] = jnp.zeros((C, C1), BF16)
-    skw[C : 2 * C, 0:C1] = jnp.zeros((C, C1), BF16)
     def widen(f, slots):
         for c in slots:
             put(xtf, f * 192 + c * 16, xt[f, c].astype(F32))
@@ -312,7 +310,8 @@
 
     get_lk.wait()
     ar_next(0, 0)
-    lax.fori_loop(0, 3 * (C // 32), fold, 0)
+    lax.fori_loop(2 * (C // 16), 3 * (C // 16), fold, 0)
+
     @pl.when(ta < 2)
     def _():
         for copy in cm_first:
@@ -337,7 +336,7 @@
         for f in (0, 1):
             widen(f, (0, 1, 10, 11))
 
-    lax.fori_loop(3 * (C // 32), 3 * (C // 16), fold, 0)
+    lax.fori_loop(C // 16, 2 * (C // 16), fold, 0)
     for copy in [get_w1] + get_affine:
         copy.wait()
 
@@ -415,17 +414,17 @@
         def _():
             to_next[f].start()
 
+    act_coarse(1)
+    act_coarse(2)
+    conv_coarse(1, 1)
+    act_coarse(3)
+    conv_coarse(1, 2)
+    conv_coarse(1, 3)
+    send_middle(1)
     act_coarse(0)
-    act_coarse(1)
-    conv_coarse(0, 0)
-    act_coarse(2)
-    conv_coarse(0, 1)
-    conv_coarse(0, 2)
+    for g in range(3):
+        conv_coarse(0, g)
     send_middle(0)
-    act_coarse(3)
-    for g in (1, 2, 3):
-        conv_coarse(1, g)
-    send_middle(1)
 
     to_second = message(17, mt.at[4:6], mt.at[0:2], near(t=2))
     by_second = message(17, mt.at[2:4], mt.at[0:2], near(t=1))
@@ -480,11 +479,45 @@
         acc2[a] = lift_part(a, 2, 4, 2)
         acc2[a, 1:2] += lift_part(a, 1, 4, 1)
 
+    lax.fori_loop(0, C // 16, fold, 0)
+    for i in range(2):
+        for dw in range(3):
+            w3[i, 3, dw, :, 0:C1] = jnp.zeros((C, C1), BF16)
+            w3[i, 0, dw, :, C1 : 2 * C1] = jnp.zeros((C, C1), BF16)
+    skw[0:C, C1 : 2 * C1] = jnp.zeros((C, C1), BF16)
+    skw[C : 2 * C, 0:C1] = jnp.zeros((C, C1), BF16)
+
     @pl.when(ta == 0)
     def _():
         for copy in cm_second:
             copy.wait_recv()
         cached_middle(2)
+
+    @pl.when(ta > 0)
+    def _():
+        to_next[1].wait_recv()
+
+    prepare(3)
+    for a in range(2):
+        acc2[a, 0:1] += lift_part(a, 1, 3, 1)
+        acc2[a, 1:2] += lift_part(a, 0, 3, 1)
+
+    @pl.when(ta > 0)
+    def _():
+        to_next[0].wait_recv()
+
+    @pl.when(ta == 2)
+    def _():
+        by_second.start()
+
+    prepare(2)
+    for a in range(2):
+        acc2[a, 0:1] += lift_part(a, 0, 2, 1)
+        lt[a, 2:4] = acc2[a].astype(BF16)
+
+    @pl.when(ta == 0)
+    def _():
+        to_second.start()
         put(cff, 0, cfb[...].astype(F32))
         for f in range(2):
             for c in range(16):
@@ -493,26 +526,6 @@
                     lt[a, f, p, :, b * C : (b + 1) * C] = take(cff, f * 512 + a * 16 + c, 32).astype(BF16)
         for copy in cf_first:
             copy.start()
-
-    @pl.when(ta > 0)
-    def _():
-        for copy in to_next:
-            copy.wait_recv()
-
-    @pl.when(ta == 2)
-    def _():
-        by_second.start()
-
-    prepare(2)
-    prepare(3)
-    for a in range(2):
-        acc2[a] += lift_part(a, 0, 2, 2)
-        acc2[a, 0:1] += lift_part(a, 1, 3, 1)
-        lt[a, 2:4] = acc2[a].astype(BF16)
-
-    @pl.when(ta == 0)
-    def _():
-        to_second.start()
 
     pivot = jnp.sum(lt[0, 2, 1, :, 0:C].astype(F32), axis=0, keepdims=True) / 16
     sums = jnp.zeros((16, C), F32)
@@ -617,12 +630,23 @@
     def fine_act_or_cached(x):
         return jnp.where(ta == 0, x, fine_act(x))
 
-    def conv_fine(dt):
-        lhs = jnp.concatenate(
-            [lf[dt : dt + 2, dw : dw + 16, :, k * C : (k + 1) * C] for k in range(4) for dw in range(3)], axis=-1
-        ).reshape(2 * 16 * 16, 12 * C)
-        part = jnp.dot(lhs, w3[dt].reshape(12 * C, 2 * C1), preferred_element_type=F32)
-        acc3[...] += part.reshape(2, 8, 2, 16, 2 * C1)
+    def conv_fine(g):
+        if g in (0, 3):
+            f = 0 if g == 0 else 1
+            lhs = jnp.concatenate(
+                [lf[g, dw : dw + 16, :, k * C : (k + 1) * C] for k in range(4) for dw in range(3)], axis=-1
+            ).reshape(16 * 16, 12 * C)
+            part = jnp.dot(lhs, w3[f].reshape(12 * C, 2 * C1), preferred_element_type=F32)
+            acc3[f] += part.reshape(8, 2, 16, 2 * C1)
+        else:
+            for a in range(2):
+                lhs = jnp.concatenate(
+                    [lf[g, dw : dw + 16, :, (a + k) * C : (a + k + 1) * C] for k in range(3) for dw in range(3)], axis=-1
+                ).reshape(16 * 16, 9 * C)
+                part = jnp.dot(lhs, wp[g - 1].reshape(9 * C, 2 * C1), preferred_element_type=F32)
+                part = part.reshape(8, 2, 16, 2 * C1)
+                for f in range(2):
+                    acc3[f, :, :, :, a * C1 : (a + 1) * C1] += part[..., f * C1 : (f + 1) * C1]
 
     def finish_fine(f):
         for c in range(16):
@@ -638,12 +662,13 @@
 
     spread_fine(0, fine_act_or_cached)
     spread_fine(1, fine_act_or_cached)
+    conv_fine(0)
     spread_fine(2, fine_act)
-    conv_fine(0)
+    conv_fine(1)
     spread_fine(3, fine_act)
-    conv_fine(1)
     conv_fine(2)
     finish_fine(0)
+    conv_fine(3)
     finish_fine(1)
 
     for copy in leave:
@@ -695,7 +720,7 @@
         V((2, 4, 2, 16, C), BF16), V((2, 4, 2, 16, C), BF16), V((4, 2, 2, 16, C), F32),
         V((4, 18, 16, 3 * C), BF16), V((2, 12, 16, C), F32),
         V((3, 3, 3, C, C), BF16), V((3, 3, 3, C, C), BF16), V((2, 3, 4 * C, 2 * C), BF16),
-        V((3, 4, 3, C, 2 * C1), BF16), V((2 * C, 2 * C1), BF16),
+        V((2, 4, 3, C, 2 * C1), BF16), V((2, 3, 3, C, 2 * C1), BF16), V((2 * C, 2 * C1), BF16),
         V((2, 12, 16, C), BF16), V((2, 2, 16, C), BF16), V((2, 2, 1, 16, 2 * C), BF16),
         V((6, 12, 16, C), BF16), V((6, 14, 16, 3 * C), BF16), V((2 * L, 256, W), F32),
         V((2, 2, 10, 16, 2 * C), F32), V((2, 4, 10, 16, 2 * C), BF16),

time: 48.8 us -> 48.4 us (level)
  no operation moved by 1% of the time
where the time goes in v4:
time: 48.4 us; the launch traced here: 48.3 us
  Pallas kernels  46.7 us (96%)
  local copies, waits for them, and re-layouts  1.67 us (3%)
    pallas_call x1, Pallas kernels, local(): pl.pallas_call(functools.partial(body, sizes), out_shape=jax.ShapeDtypeSt...  46.7 us
    unnamed x1, local copies, waits for them, and re-layouts  1.67 us

profile of v4, /device:TPU:1, one launch (start us, length us, event | category | flops | bytes accessed | tf_op | source)
XLA Modules:
  0.0 48.3 jit_solution(12081732303676160361)
XLA Ops:
  0.0 46.7 %shard_map.118 = bf16[1024,128]{1,0:T(8,128)(2,1)} custom-call(bf16[256,256]{1,0:T(8,128)(2,1)} %bitcast.11, bf16[256,256]{1,0:T(8,128)(2,1)} %bitcast.12, bf16[256,256]{1,0:T(8,128)(2,1)} %bitcast.13, bf16[1024,256]{1,0:T(8,128)(2,1)} %bitcast.10, f32[1,256]{1,0:T(1,128)} %bitcast.14, f32[1,256]{1,0:T(1,128)} %bitcast.15, f32[1,256]{1,0:T(1,128)} %bitcast.16, ...), custom_call_target="tpu_custom_call" | custom-call | tf_op jit(solution)/shard_map/pallas_call | solution.py:733
  46.7 1.7 %copy.14 = bf16[2,32,16,128]{3,2,1,0:T(8,128)(2,1)} copy(bf16[2,32,16,128]{3,2,1,0:T(8,128)(2,1)} %bitcast.9) | data formatting | bytes 524288

commit v5 on v4

--- a/solution.py
+++ b/solution.py
@@ -37,7 +37,7 @@
     coarse_gain, coarse_shift, fine_gain, fine_shift,
     coarse_kernel, lift_kernel, fine_kernel, skip_kernel,
     out_ref, affine,
-    cb, cbp, cmb, cfb, xf, cff, xt, xtf, ss, sr, saf, act_a, acc1, w1, lk, w2, w3, wp, skw,
+    cb, cbp, cmb, cfb, xf, cff, xt, xtf, ss, sr, saf, act_a, acc1, w1, lk, w2, w3, skw,
     cm, cs, cfs, mt, mid_g, gf, acc2, lt, lf, acc3, back, outb, ar_src, ar_recv,
     local_sem, ar_send, ar_got, send_sem, recv_sem,
 ):
@@ -158,7 +158,7 @@
         return [
             pltpu.make_async_remote_copy(
                 src_ref=ar_src.at[which, stage], dst_ref=ar_recv.at[which, base + i],
-                send_sem=ar_send.at[which, base + i], recv_sem=ar_got.at[which, base + i],
+                send_sem=ar_send.at[which, stage], recv_sem=ar_got.at[which, stage],
                 device_id=peer, device_id_type=MESH,
             )
             for i, peer in enumerate(peers)
@@ -168,11 +168,15 @@
         for copy in ar_copies(which, stage):
             copy.start()
 
+    def ar_all(which, stage, sem):
+        peers, base = stages[stage]
+        slots = ar_recv.at[which, base : base + len(peers)]
+        return pltpu.make_async_copy(slots, slots, sem.at[which, stage])
+
     def ar_finish(which, stage):
         peers, base = stages[stage]
         n = len(peers) + 1
-        for copy in ar_copies(which, stage):
-            copy.wait_recv()
+        ar_all(which, stage, ar_got).wait()
         tiles = [ar_src[which, stage]] + [ar_recv[which, base + i] for i in range(n - 1)]
         average = functools.reduce(jnp.add, tiles) / n
         spread = functools.reduce(jnp.add, [(tile - average) * (tile - average) for tile in tiles]) / n
@@ -217,11 +221,7 @@
     get_cm = load(cache_middle_hbm, cmb)
     get_w1 = load(coarse_kernel, w1)
     get_affine = [load(ref, affine.at[i]) for i, ref in enumerate((coarse_gain, coarse_shift, fine_gain, fine_shift))]
-    get_w3 = [
-        load(fine_kernel.at[2 * i], w3.at[i, a : a + 3, :, :, a * C1 : (a + 1) * C1]) for i in range(2) for a in range(2)
-    ] + [
-        load(fine_kernel.at[1 + i - f], wp.at[i, :, :, :, f * C1 : (f + 1) * C1]) for i in range(2) for f in range(2)
-    ]
+    get_w3 = [load(fine_kernel, w3.at[:, a : a + 3, :, :, a * C1 : (a + 1) * C1]) for a in range(2)]
     get_skip = [load(skip_kernel, skw.at[a * C : (a + 1) * C, a * C1 : (a + 1) * C1]) for a in range(2)]
     get_cf = load(cache_fine_hbm, cfb)
 
@@ -352,16 +352,17 @@
             outside = first_h if side == 0 else last_h
             for k in range(2):
                 x = sr[side, f, k].astype(F32)
-                y = jnp.where(raw, x, act(x)) if f < 2 else act(x)
+                y = jnp.where(raw, x, act(x))
                 gone = jnp.logical_or(jnp.logical_and(first_w, cols < 2), jnp.logical_and(last_w, cols >= 10))
                 saf[f, side, k] = jnp.where(jnp.logical_or(outside, gone), 0.0, y)
 
-    def act_coarse(f):
+    def act_coarse(f, carry):
         strips_of(f)
+        raw = jnp.logical_and(ta == 0, f < 2)
         for c in range(12):
-            at = f * 192 + c * 16
+            at = pl.multiple_of(f * 192 + c * 16, 16)
             x = take(xtf, at)
-            x = jnp.where(ta == 0, x, act(x)) if f < 2 else act(x)
+            x = jnp.where(raw, x, act(x))
             if c < 2:
                 x = jnp.where(first_w, 0.0, x)
             if c >= 10:
@@ -378,6 +379,7 @@
             for dw in range(3):
                 for dh in range(3):
                     act_a[f, 12 + 2 * dw + side, :, dh * C : (dh + 1) * C] = rolled(lines[dh], -dw).astype(BF16)
+        return carry
 
     def conv_coarse(f, g):
         lhs = jnp.concatenate(
@@ -389,7 +391,7 @@
             axis=-1,
         ).reshape(12 * 16, 9 * C)
         part = jnp.dot(lhs, w1[g - f].reshape(9 * C, C), preferred_element_type=F32).reshape(12, 16, C)
-        acc1[f] = part if g == f else acc1[f] + part
+        acc1[f] += part
 
     def finish_middle(f):
         for c in range(10):
@@ -414,49 +416,43 @@
         def _():
             to_next[f].start()
 
-    act_coarse(1)
-    act_coarse(2)
-    conv_coarse(1, 1)
-    act_coarse(3)
-    conv_coarse(1, 2)
-    conv_coarse(1, 3)
-    send_middle(1)
-    act_coarse(0)
-    for g in range(3):
-        conv_coarse(0, g)
-    send_middle(0)
+    lax.fori_loop(0, 4, act_coarse, 0)
+    acc1[...] = jnp.zeros_like(acc1)
+    for f in (1, 0):
+
+        def conv_step(dt, carry, f=f):
+            conv_coarse(f, dt + f)
+            return carry
+
+        lax.fori_loop(0, 3, conv_step, 0)
+        send_middle(f)
 
     to_second = message(17, mt.at[4:6], mt.at[0:2], near(t=2))
     by_second = message(17, mt.at[2:4], mt.at[0:2], near(t=1))
 
-    def prepare(g):
+    def prepare(g, carry=0):
         top = mt[g, 10].astype(F32)
         bottom = mt[g, 11].astype(F32)
         for c in range(10):
             x = mt[g, c].astype(F32)
             put(gf, 16 * c, x)
-            mid_g[g, c, :, 0:C] = jnp.where(row16 == 0, top[c : c + 1], rolled(x, 1)).astype(BF16)
-            mid_g[g, c, :, C : 2 * C] = mt[g, c]
-            mid_g[g, c, :, 2 * C : 3 * C] = jnp.where(row16 == 15, bottom[c : c + 1], rolled(x, -1)).astype(BF16)
+            mid_g[0, g, c, :, 0:C] = jnp.where(row16 == 0, top[c : c + 1], rolled(x, 1)).astype(BF16)
+            mid_g[0, g, c, :, C : 2 * C] = mt[g, c]
+            mid_g[1, g, c, :, 0:C] = mt[g, c]
+            mid_g[1, g, c, :, C : 2 * C] = jnp.where(row16 == 15, bottom[c : c + 1], rolled(x, -1)).astype(BF16)
         row_top = take(gf, 0, 16, half)
         row_bottom = take(gf, 15, 16, half)
         for j in range(2):
-            mid_g[g, 10 + j, :, 0:C] = rolled(row_bottom, -j).astype(BF16)
-            mid_g[g, 10 + j, :, C : 2 * C] = rolled(bottom, -j).astype(BF16)
-            mid_g[g, 12 + j, :, C : 2 * C] = rolled(top, -j).astype(BF16)
-            mid_g[g, 12 + j, :, 2 * C : 3 * C] = rolled(row_top, -j).astype(BF16)
+            mid_g[0, g, 10 + j, :, 0:C] = rolled(row_bottom, -j).astype(BF16)
+            mid_g[0, g, 10 + j, :, C : 2 * C] = rolled(bottom, -j).astype(BF16)
+            mid_g[1, g, 10 + j, :, 0:C] = rolled(top, -j).astype(BF16)
+            mid_g[1, g, 10 + j, :, C : 2 * C] = rolled(row_top, -j).astype(BF16)
+        return carry
 
     def lift_part(a, dt, g, frames):
-        lanes = slice(a * C, (a + 2) * C)
+        at = pl.ds(g, frames)
         lhs = jnp.concatenate(
-            [
-                jnp.concatenate(
-                    [mid_g[g : g + frames, j : j + 9, :, lanes], mid_g[g : g + frames, 10 + 2 * a + j : 11 + 2 * a + j, :, lanes]],
-                    axis=1,
-                )
-                for j in range(2)
-            ],
-            axis=-1,
+            [jnp.concatenate([mid_g[a, at, j : j + 9], mid_g[a, at, 10 + j : 11 + j]], axis=1) for j in range(2)], axis=-1
         ).reshape(frames * 10 * 16, 4 * C)
         part = jnp.dot(lhs, w2[a, dt], preferred_element_type=F32)
         return part.reshape(frames, 10, 16, 2 * C)
@@ -473,14 +469,15 @@
 
     for copy in get_w3 + get_skip + [get_cf]:
         copy.wait()
-    prepare(4)
-    prepare(5)
-    for a in range(2):
+    lax.fori_loop(4, 6, prepare, 0)
+
+    @pl.loop(0, 2)
+    def _(a):
         acc2[a] = lift_part(a, 2, 4, 2)
         acc2[a, 1:2] += lift_part(a, 1, 4, 1)
 
     lax.fori_loop(0, C // 16, fold, 0)
-    for i in range(2):
+    for i in range(3):
         for dw in range(3):
             w3[i, 3, dw, :, 0:C1] = jnp.zeros((C, C1), BF16)
             w3[i, 0, dw, :, C1 : 2 * C1] = jnp.zeros((C, C1), BF16)
@@ -498,9 +495,11 @@
         to_next[1].wait_recv()
 
     prepare(3)
-    for a in range(2):
-        acc2[a, 0:1] += lift_part(a, 1, 3, 1)
-        acc2[a, 1:2] += lift_part(a, 0, 3, 1)
+
+    @pl.loop(0, 4)
+    def _(i):
+        a, out = i // 2, lax.rem(i, 2)
+        acc2[a, pl.ds(out, 1)] += lift_part(a, 1 - out, 3, 1)
 
     @pl.when(ta > 0)
     def _():
@@ -511,7 +510,9 @@
         by_second.start()
 
     prepare(2)
-    for a in range(2):
+
+    @pl.loop(0, 2)
+    def _(a):
         acc2[a, 0:1] += lift_part(a, 0, 2, 1)
         lt[a, 2:4] = acc2[a].astype(BF16)
 
@@ -545,17 +546,11 @@
     ar_src[1, 0, 1:2, :] = jnp.maximum(jnp.sum(squares, axis=0, keepdims=True) / count - off * off, 0.0)
     ar_start(1, 0)
 
-    def lift_before_new(a):
-        acc2[a] = lift_part(a, 2, 2, 2)
-
-    def lift_before_old(a):
-        acc2[a] += lift_part(a, 0, 0, 2)
-        lt[a, 0:2] = (acc2[a] + lift_part(a, 1, 1, 2)).astype(BF16)
-
     @pl.when(ta > 0)
     def _():
-        lift_before_new(0)
-        lift_before_new(1)
+        @pl.loop(0, 2)
+        def _(a):
+            acc2[a] = lift_part(a, 2, 2, 2)
 
     @pl.when(ta == 0)
     def _():
@@ -588,15 +583,48 @@
 
     @pl.when(ta > 0)
     def _():
-        prepare(0)
-        prepare(1)
-        lift_before_old(0)
-        lift_before_old(1)
-
+        lax.fori_loop(0, 2, prepare, 0)
+
+        @pl.loop(0, 4)
+        def _(i):
+            a, dt = i // 2, lax.rem(i, 2)
+            acc2[a] += lift_part(a, dt, dt, 2)
+
+        for a in range(2):
+            lt[a, 0:2] = acc2[a].astype(BF16)
+
+    for stage in range(2):
+        ar_all(0, stage, ar_send).wait()
+    for copy in cols_own + rows_own:
+        copy.wait_send()
+
+    @pl.when(ta < 2)
+    def _():
+        for copy in cm_first + cm_second:
+            copy.wait_send()
+
+    @pl.when(ta == 0)
+    def _():
+        for copy in cols_cached + rows_cached + cf_first + cf_second:
+            copy.wait_send()
+
+    @pl.when(ta < nt - 1)
+    def _():
+        for copy in [center] + cols_next + rows_next + to_next:
+            copy.wait_send()
+
+    @pl.when(jnp.logical_or(ta == 0, ta == 2))
+    def _():
+        to_second.wait_send()
 
     lane = lax.broadcasted_iota(jnp.int32, (16, 2 * C), 1)
 
-    def spread_fine(f, fn):
+    def spread_fine(f, carry):
+        raw = jnp.logical_and(ta == 0, f < 2)
+
+        def fn(x):
+            return jnp.where(raw, x, fine_act(x))
+
         top = jnp.where(first_h, 0.0, fn(lt[1, f, 9].astype(F32)))
         bottom = jnp.where(last_h, 0.0, fn(lt[0, f, 9].astype(F32)))
         for p in range(9):
@@ -612,6 +640,7 @@
                 part = part.astype(BF16)
                 for b in range(2):
                     lf[f, 2 * p + b, :, k * C : (k + 1) * C] = part[:, b * C : (b + 1) * C]
+        return carry
 
     @pl.when(ta == 0)
     def _():
@@ -627,26 +656,14 @@
         half = (x - mean2) * scale2 + shift2
         return half + half * jnp.tanh(half)
 
-    def fine_act_or_cached(x):
-        return jnp.where(ta == 0, x, fine_act(x))
-
-    def conv_fine(g):
-        if g in (0, 3):
-            f = 0 if g == 0 else 1
-            lhs = jnp.concatenate(
-                [lf[g, dw : dw + 16, :, k * C : (k + 1) * C] for k in range(4) for dw in range(3)], axis=-1
-            ).reshape(16 * 16, 12 * C)
-            part = jnp.dot(lhs, w3[f].reshape(12 * C, 2 * C1), preferred_element_type=F32)
-            acc3[f] += part.reshape(8, 2, 16, 2 * C1)
-        else:
-            for a in range(2):
-                lhs = jnp.concatenate(
-                    [lf[g, dw : dw + 16, :, (a + k) * C : (a + k + 1) * C] for k in range(3) for dw in range(3)], axis=-1
-                ).reshape(16 * 16, 9 * C)
-                part = jnp.dot(lhs, wp[g - 1].reshape(9 * C, 2 * C1), preferred_element_type=F32)
-                part = part.reshape(8, 2, 16, 2 * C1)
-                for f in range(2):
-                    acc3[f, :, :, :, a * C1 : (a + 1) * C1] += part[..., f * C1 : (f + 1) * C1]
+    def conv_fine(dt, carry):
+        at = pl.ds(dt, 2)
+        lhs = jnp.concatenate(
+            [lf[at, dw : dw + 16, :, k * C : (k + 1) * C] for k in range(4) for dw in range(3)], axis=-1
+        ).reshape(2 * 16 * 16, 12 * C)
+        part = jnp.dot(lhs, w3[dt].reshape(12 * C, 2 * C1), preferred_element_type=F32)
+        acc3[...] += part.reshape(2, 8, 2, 16, 2 * C1)
+        return carry
 
     def finish_fine(f):
         for c in range(16):
@@ -660,44 +677,15 @@
         for f in range(2)
     ]
 
-    spread_fine(0, fine_act_or_cached)
-    spread_fine(1, fine_act_or_cached)
-    conv_fine(0)
-    spread_fine(2, fine_act)
-    conv_fine(1)
-    spread_fine(3, fine_act)
-    conv_fine(2)
+    lax.fori_loop(0, 4, spread_fine, 0)
+    lax.fori_loop(0, 3, conv_fine, 0)
     finish_fine(0)
-    conv_fine(3)
     finish_fine(1)
 
     for copy in leave:
         copy.wait()
-    for which in range(2):
-        for stage in range(2):
-            for copy in ar_copies(which, stage):
-                copy.wait_send()
-    for copy in cols_own + rows_own:
-        copy.wait_send()
-
-    @pl.when(ta < 2)
-    def _():
-        for copy in cm_first + cm_second:
-            copy.wait_send()
-
-    @pl.when(ta == 0)
-    def _():
-        for copy in cols_cached + rows_cached + cf_first + cf_second:
-            copy.wait_send()
-
-    @pl.when(ta < nt - 1)
-    def _():
-        for copy in [center] + cols_next + rows_next + to_next:
-            copy.wait_send()
-
-    @pl.when(jnp.logical_or(ta == 0, ta == 2))
-    def _():
-        to_second.wait_send()
+    for stage in range(2):
+        ar_all(1, stage, ar_send).wait()
 
 
 def local(
@@ -720,14 +708,14 @@
         V((2, 4, 2, 16, C), BF16), V((2, 4, 2, 16, C), BF16), V((4, 2, 2, 16, C), F32),
         V((4, 18, 16, 3 * C), BF16), V((2, 12, 16, C), F32),
         V((3, 3, 3, C, C), BF16), V((3, 3, 3, C, C), BF16), V((2, 3, 4 * C, 2 * C), BF16),
-        V((2, 4, 3, C, 2 * C1), BF16), V((2, 3, 3, C, 2 * C1), BF16), V((2 * C, 2 * C1), BF16),
+        V((3, 4, 3, C, 2 * C1), BF16), V((2 * C, 2 * C1), BF16),
         V((2, 12, 16, C), BF16), V((2, 2, 16, C), BF16), V((2, 2, 1, 16, 2 * C), BF16),
-        V((6, 12, 16, C), BF16), V((6, 14, 16, 3 * C), BF16), V((2 * L, 256, W), F32),
+        V((6, 12, 16, C), BF16), V((2, 6, 12, 16, 2 * C), BF16), V((2 * L, 256, W), F32),
         V((2, 2, 10, 16, 2 * C), F32), V((2, 4, 10, 16, 2 * C), BF16),
         V((4, 18, 16, 4 * C), BF16), V((2, 8, 2, 16, 2 * C1), F32), V((1024, C1), F32), V((1024, C1), BF16),
         V((2, 2, 8, C), F32), V((2, peers, 8, C), F32),
         pltpu.SemaphoreType.DMA((60,)),
-        pltpu.SemaphoreType.DMA((2, peers)), pltpu.SemaphoreType.DMA((2, peers)),
+        pltpu.SemaphoreType.DMA((2, 2)), pltpu.SemaphoreType.DMA((2, 2)),
         pltpu.SemaphoreType.DMA((24,)), pltpu.SemaphoreType.DMA((24,)),
     ]
     decoded = pl.pallas_call(

time: 48.4 us -> 49 us (1.012)
  Pallas kernels: 46.7 us -> 47.2 us
    pallas_call x1, Pallas kernels: 46.7 us -> 47.2 us  [local(): pl.pallas_call(functools.partial(body, sizes), out_shape=jax.ShapeDtypeSt...]
where the time goes in v5:
time: 49 us; the launch traced here: 48.9 us
  Pallas kernels  47.2 us (96%)
  local copies, waits for them, and re-layouts  1.67 us (3%)
    pallas_call x1, Pallas kernels, local(): pl.pallas_call(functools.partial(body, sizes), out_shape=jax.ShapeDtypeSt...  47.2 us
    unnamed x1, local copies, waits for them, and re-layouts  1.67 us

profile of v5, /device:TPU:1, one launch (start us, length us, event | category | flops | bytes accessed | tf_op | source)
XLA Modules:
  0.0 48.9 jit_solution(13392437840032566350)
XLA Ops:
  0.0 47.2 %shard_map.118 = bf16[1024,128]{1,0:T(8,128)(2,1)} custom-call(bf16[256,256]{1,0:T(8,128)(2,1)} %bitcast.11, bf16[256,256]{1,0:T(8,128)(2,1)} %bitcast.12, bf16[256,256]{1,0:T(8,128)(2,1)} %bitcast.13, bf16[1024,256]{1,0:T(8,128)(2,1)} %bitcast.10, f32[1,256]{1,0:T(1,128)} %bitcast.14, f32[1,256]{1,0:T(1,128)} %bitcast.15, f32[1,256]{1,0:T(1,128)} %bitcast.16, ...), custom_call_target="tpu_custom_call" | custom-call | tf_op jit(solution)/shard_map/pallas_call | solution.py:721
  47.2 1.7 %copy.14 = bf16[2,32,16,128]{3,2,1,0:T(8,128)(2,1)} copy(bf16[2,32,16,128]{3,2,1,0:T(8,128)(2,1)} %bitcast.9) | data formatting | bytes 524288

commit v6 on v4

--- a/solution.py
+++ b/solution.py
@@ -38,7 +38,7 @@
     coarse_kernel, lift_kernel, fine_kernel, skip_kernel,
     out_ref, affine,
     cb, cbp, cmb, cfb, xf, cff, xt, xtf, ss, sr, saf, act_a, acc1, w1, lk, w2, w3, wp, skw,
-    cm, cs, cfs, mt, mid_g, gf, acc2, lt, lf, acc3, back, outb, ar_src, ar_recv,
+    cm, cs, cfs, mt, mid_g, gf, acc2, lt, ltp, lf, acc3, back, outb, ar_src, ar_recv,
     local_sem, ar_send, ar_got, send_sem, recv_sem,
 ):
     nt, nh, nw, C, C1 = sizes
@@ -158,7 +158,7 @@
         return [
             pltpu.make_async_remote_copy(
                 src_ref=ar_src.at[which, stage], dst_ref=ar_recv.at[which, base + i],
-                send_sem=ar_send.at[which, base + i], recv_sem=ar_got.at[which, base + i],
+                send_sem=ar_send.at[which, stage], recv_sem=ar_got.at[which, stage],
                 device_id=peer, device_id_type=MESH,
             )
             for i, peer in enumerate(peers)
@@ -168,11 +168,15 @@
         for copy in ar_copies(which, stage):
             copy.start()
 
+    def ar_all(which, stage, sem):
+        peers, base = stages[stage]
+        slots = ar_recv.at[which, base : base + len(peers)]
+        return pltpu.make_async_copy(slots, slots, sem.at[which, stage])
+
     def ar_finish(which, stage):
         peers, base = stages[stage]
         n = len(peers) + 1
-        for copy in ar_copies(which, stage):
-            copy.wait_recv()
+        ar_all(which, stage, ar_got).wait()
         tiles = [ar_src[which, stage]] + [ar_recv[which, base + i] for i in range(n - 1)]
         average = functools.reduce(jnp.add, tiles) / n
         spread = functools.reduce(jnp.add, [(tile - average) * (tile - average) for tile in tiles]) / n
@@ -310,7 +314,7 @@
 
     get_lk.wait()
     ar_next(0, 0)
-    lax.fori_loop(2 * (C // 16), 3 * (C // 16), fold, 0)
+    lax.fori_loop(3 * (C // 32), 3 * (C // 16), fold, 0)
 
     @pl.when(ta < 2)
     def _():
@@ -336,7 +340,7 @@
         for f in (0, 1):
             widen(f, (0, 1, 10, 11))
 
-    lax.fori_loop(C // 16, 2 * (C // 16), fold, 0)
+    lax.fori_loop(0, 3 * (C // 32), fold, 0)
     for copy in [get_w1] + get_affine:
         copy.wait()
 
@@ -479,7 +483,6 @@
         acc2[a] = lift_part(a, 2, 4, 2)
         acc2[a, 1:2] += lift_part(a, 1, 4, 1)
 
-    lax.fori_loop(0, C // 16, fold, 0)
     for i in range(2):
         for dw in range(3):
             w3[i, 3, dw, :, 0:C1] = jnp.zeros((C, C1), BF16)
@@ -550,7 +553,7 @@
 
     def lift_before_old(a):
         acc2[a] += lift_part(a, 0, 0, 2)
-        lt[a, 0:2] = (acc2[a] + lift_part(a, 1, 1, 2)).astype(BF16)
+        ltp[a] = (acc2[a] + lift_part(a, 1, 1, 2)).astype(BF16)
 
     @pl.when(ta > 0)
     def _():
@@ -586,22 +589,46 @@
     def _():
         to_second.wait_recv()
 
-    @pl.when(ta > 0)
-    def _():
-        prepare(0)
-        prepare(1)
-        lift_before_old(0)
-        lift_before_old(1)
-
+    prepare(0)
+    prepare(1)
+
+    for stage in range(2):
+        ar_all(0, stage, ar_send).wait()
+    for copy in cols_own + rows_own:
+        copy.wait_send()
+
+    @pl.when(ta < 2)
+    def _():
+        for copy in cm_first + cm_second:
+            copy.wait_send()
+
+    @pl.when(ta == 0)
+    def _():
+        for copy in cols_cached + rows_cached + cf_first + cf_second:
+            copy.wait_send()
+
+    @pl.when(ta < nt - 1)
+    def _():
+        for copy in [center] + cols_next + rows_next + to_next:
+            copy.wait_send()
+
+    @pl.when(jnp.logical_or(ta == 0, ta == 2))
+    def _():
+        to_second.wait_send()
 
     lane = lax.broadcasted_iota(jnp.int32, (16, 2 * C), 1)
 
-    def spread_fine(f, fn):
-        top = jnp.where(first_h, 0.0, fn(lt[1, f, 9].astype(F32)))
-        bottom = jnp.where(last_h, 0.0, fn(lt[0, f, 9].astype(F32)))
+    def fine_cells(a, f, p):
+        if f < 2:
+            return jnp.where(ta == 0, lt[a, f, p].astype(F32), fine_act(ltp[a, f, p].astype(F32)))
+        return fine_act(lt[a, f, p].astype(F32))
+
+    def spread_fine(f):
+        top = jnp.where(first_h, 0.0, fine_cells(1, f, 9))
+        bottom = jnp.where(last_h, 0.0, fine_cells(0, f, 9))
         for p in range(9):
-            even = fn(lt[0, f, p].astype(F32))
-            odd = fn(lt[1, f, p].astype(F32))
+            even = fine_cells(0, f, p)
+            odd = fine_cells(1, f, p)
             before = jnp.where(row16w == 0, top[p : p + 1], rolled(odd, 1))
             after = jnp.where(row16w == 15, bottom[p : p + 1], rolled(even, -1))
             for k, part in enumerate((before, even, odd, after)):
@@ -626,9 +653,6 @@
     def fine_act(x):
         half = (x - mean2) * scale2 + shift2
         return half + half * jnp.tanh(half)
-
-    def fine_act_or_cached(x):
-        return jnp.where(ta == 0, x, fine_act(x))
 
     def conv_fine(g):
         if g in (0, 3):
@@ -660,44 +684,23 @@
         for f in range(2)
     ]
 
-    spread_fine(0, fine_act_or_cached)
-    spread_fine(1, fine_act_or_cached)
+    spread_fine(2)
+    lift_before_old(0)
+    spread_fine(3)
+    lift_before_old(1)
+    conv_fine(3)
+    spread_fine(0)
+    conv_fine(2)
+    spread_fine(1)
+    conv_fine(1)
+    finish_fine(1)
     conv_fine(0)
-    spread_fine(2, fine_act)
-    conv_fine(1)
-    spread_fine(3, fine_act)
-    conv_fine(2)
     finish_fine(0)
-    conv_fine(3)
-    finish_fine(1)
 
     for copy in leave:
         copy.wait()
-    for which in range(2):
-        for stage in range(2):
-            for copy in ar_copies(which, stage):
-                copy.wait_send()
-    for copy in cols_own + rows_own:
-        copy.wait_send()
-
-    @pl.when(ta < 2)
-    def _():
-        for copy in cm_first + cm_second:
-            copy.wait_send()
-
-    @pl.when(ta == 0)
-    def _():
-        for copy in cols_cached + rows_cached + cf_first + cf_second:
-            copy.wait_send()
-
-    @pl.when(ta < nt - 1)
-    def _():
-        for copy in [center] + cols_next + rows_next + to_next:
-            copy.wait_send()
-
-    @pl.when(jnp.logical_or(ta == 0, ta == 2))
-    def _():
-        to_second.wait_send()
+    for stage in range(2):
+        ar_all(1, stage, ar_send).wait()
 
 
 def local(
@@ -723,11 +726,11 @@
         V((2, 4, 3, C, 2 * C1), BF16), V((2, 3, 3, C, 2 * C1), BF16), V((2 * C, 2 * C1), BF16),
         V((2, 12, 16, C), BF16), V((2, 2, 16, C), BF16), V((2, 2, 1, 16, 2 * C), BF16),
         V((6, 12, 16, C), BF16), V((6, 14, 16, 3 * C), BF16), V((2 * L, 256, W), F32),
-        V((2, 2, 10, 16, 2 * C), F32), V((2, 4, 10, 16, 2 * C), BF16),
+        V((2, 2, 10, 16, 2 * C), F32), V((2, 4, 10, 16, 2 * C), BF16), V((2, 2, 10, 16, 2 * C), BF16),
         V((4, 18, 16, 4 * C), BF16), V((2, 8, 2, 16, 2 * C1), F32), V((1024, C1), F32), V((1024, C1), BF16),
         V((2, 2, 8, C), F32), V((2, peers, 8, C), F32),
         pltpu.SemaphoreType.DMA((60,)),
-        pltpu.SemaphoreType.DMA((2, peers)), pltpu.SemaphoreType.DMA((2, peers)),
+        pltpu.SemaphoreType.DMA((2, 2)), pltpu.SemaphoreType.DMA((2, 2)),
         pltpu.SemaphoreType.DMA((24,)), pltpu.SemaphoreType.DMA((24,)),
     ]
     decoded = pl.pallas_call(

time: 48.4 us -> 47.7 us (0.986)
  Pallas kernels: 46.7 us -> 45.9 us
    pallas_call x1, Pallas kernels: 46.7 us -> 45.9 us  [local(): pl.pallas_call(functools.partial(body, sizes), out_shape=jax.ShapeDtypeSt...]
where the time goes in v6:
time: 47.7 us; the launch traced here: 47.6 us
  Pallas kernels  45.9 us (96%)
  local copies, waits for them, and re-layouts  1.67 us (4%)
    pallas_call x1, Pallas kernels, local(): pl.pallas_call(functools.partial(body, sizes), out_shape=jax.ShapeDtypeSt...  45.9 us
    unnamed x1, local copies, waits for them, and re-layouts  1.67 us

profile of v6, /device:TPU:1, one launch (start us, length us, event | category | flops | bytes accessed | tf_op | source)
XLA Modules:
  0.0 47.6 jit_solution(10094815673514340251)
XLA Ops:
  0.0 45.9 %shard_map.118 = bf16[1024,128]{1,0:T(8,128)(2,1)} custom-call(bf16[256,256]{1,0:T(8,128)(2,1)} %bitcast.11, bf16[256,256]{1,0:T(8,128)(2,1)} %bitcast.12, bf16[256,256]{1,0:T(8,128)(2,1)} %bitcast.13, bf16[1024,256]{1,0:T(8,128)(2,1)} %bitcast.10, f32[1,256]{1,0:T(1,128)} %bitcast.14, f32[1,256]{1,0:T(1,128)} %bitcast.15, f32[1,256]{1,0:T(1,128)} %bitcast.16, ...), custom_call_target="tpu_custom_call" | custom-call | tf_op jit(solution)/shard_map/pallas_call | solution.py:736
  46.0 1.7 %copy.14 = bf16[2,32,16,128]{3,2,1,0:T(8,128)(2,1)} copy(bf16[2,32,16,128]{3,2,1,0:T(8,128)(2,1)} %bitcast.9) | data formatting | bytes 524288

commit v7 on v6

--- a/solution.py
+++ b/solution.py
@@ -328,23 +328,11 @@
         for copy in cm_second:
             copy.start()
 
-    @pl.when(ta > 0)
-    def _():
-        center.wait_recv()
-        put(xf, 0, cbp[...].astype(F32))
-        for f in range(2):
-            for c in range(8):
-                put(xtf, f * 192 + (2 + c) * 16, take(xf, f * 128 + c, 8))
-        for copy in cols_next:
-            copy.wait_recv()
-        for f in (0, 1):
-            widen(f, (0, 1, 10, 11))
-
     lax.fori_loop(0, 3 * (C // 32), fold, 0)
     for copy in [get_w1] + get_affine:
         copy.wait()
 
-    for copy in rows_own + rows_next:
+    for copy in rows_own:
         copy.wait_recv()
     act, *_ = normaliser(0, affine[0], affine[1])
 
@@ -393,7 +381,7 @@
             axis=-1,
         ).reshape(12 * 16, 9 * C)
         part = jnp.dot(lhs, w1[g - f].reshape(9 * C, C), preferred_element_type=F32).reshape(12, 16, C)
-        acc1[f] = part if g == f else acc1[f] + part
+        acc1[f] = part if g == 2 else acc1[f] + part
 
     def finish_middle(f):
         for c in range(10):
@@ -418,16 +406,33 @@
         def _():
             to_next[f].start()
 
-    act_coarse(1)
     act_coarse(2)
-    conv_coarse(1, 1)
     act_coarse(3)
     conv_coarse(1, 2)
+    conv_coarse(0, 2)
     conv_coarse(1, 3)
+
+    @pl.when(ta > 0)
+    def _():
+        center.wait_recv()
+        put(xf, 0, cbp[...].astype(F32))
+        for f in range(2):
+            for c in range(8):
+                put(xtf, f * 192 + (2 + c) * 16, take(xf, f * 128 + c, 8))
+        for copy in cols_next:
+            copy.wait_recv()
+        for f in (0, 1):
+            widen(f, (0, 1, 10, 11))
+
+    for copy in rows_next:
+        copy.wait_recv()
+
+    act_coarse(1)
+    conv_coarse(1, 1)
     send_middle(1)
     act_coarse(0)
-    for g in range(3):
-        conv_coarse(0, g)
+    conv_coarse(0, 1)
+    conv_coarse(0, 0)
     send_middle(0)
 
     to_second = message(17, mt.at[4:6], mt.at[0:2], near(t=2))

time: 47.7 us -> 47.4 us (level)
  no operation moved by 1% of the time
where the time goes in v7:
time: 47.4 us; the launch traced here: 47.3 us
  Pallas kernels  45.6 us (96%)
  local copies, waits for them, and re-layouts  1.67 us (4%)
    pallas_call x1, Pallas kernels, local(): pl.pallas_call(functools.partial(body, sizes), out_shape=jax.ShapeDtypeSt...  45.6 us
    unnamed x1, local copies, waits for them, and re-layouts  1.67 us

profile of v7, /device:TPU:1, one launch (start us, length us, event | category | flops | bytes accessed | tf_op | source)
XLA Modules:
  0.0 47.3 jit_solution(3562402391767909895)
XLA Ops:
  0.0 45.6 %shard_map.118 = bf16[1024,128]{1,0:T(8,128)(2,1)} custom-call(bf16[256,256]{1,0:T(8,128)(2,1)} %bitcast.11, bf16[256,256]{1,0:T(8,128)(2,1)} %bitcast.12, bf16[256,256]{1,0:T(8,128)(2,1)} %bitcast.13, bf16[1024,256]{1,0:T(8,128)(2,1)} %bitcast.10, f32[1,256]{1,0:T(1,128)} %bitcast.14, f32[1,256]{1,0:T(1,128)} %bitcast.15, f32[1,256]{1,0:T(1,128)} %bitcast.16, ...), custom_call_target="tpu_custom_call" | custom-call | tf_op jit(solution)/shard_map/pallas_call | solution.py:741
  45.6 1.7 %copy.14 = bf16[2,32,16,128]{3,2,1,0:T(8,128)(2,1)} copy(bf16[2,32,16,128]{3,2,1,0:T(8,128)(2,1)} %bitcast.9) | data formatting | bytes 524288
